TPU v7x, 512 devices: a whole 4x8x8 slice. The times are simulated.
512 devices in a mesh: xy: 128 (over y, z, core), gz: 4 (over x).
Axes of the slice: x: 4, y: 8, z: 8, core: 2. Of those that a mesh axis runs over, the one named last changes fastest.
Arguments:
- material: int32 [16, 2048, 256], P('gz', 'xy'), may hold values from 0 to 7
- diffusivity: float32 [8], replicated, may hold values from 0.2 to 5
- variation: float32 [16, 2048, 256], P('gz', 'xy'), may hold values from 0.5 to 2
Outputs:
- stencil: float32 [27, 8, 1024, 128], P(None, 'gz', 'xy')
Inputs may be any that keep to these rules, and one draw needn't show every extreme that they name: Each fine cell's material number is an integer from 0 to 7.
All inputs are finite; a program needn't handle non-finite values.
Results may differ from a plain program's by a relative error of at most 0.0003.
Values sent between devices are 32-bit elements; how exact they have to be, the bound alone decides.
A program may use at most 64 MiB of HBM per device.

v0:
```python
import jax
import jax.numpy as jnp
from jax import lax
from jax.sharding import PartitionSpec as P

NMAT = 8


def with_halo(block, sides, width):
    for axis, dim in sides:
        count = lax.axis_size(axis)
        forward = [(i, i + 1) for i in range(count - 1)]
        backward = [(target, source) for source, target in forward]
        low = lax.ppermute(
            lax.slice_in_dim(block, block.shape[dim] - width, None, axis=dim), axis, forward
        )
        high = lax.ppermute(lax.slice_in_dim(block, 0, width, axis=dim), axis, backward)
        block = jnp.concatenate([low, block, high], axis=dim)
    return block


def passed_along(value, axis, steps):
    count = lax.axis_size(axis)
    first, last = (max(0, -steps), min(count, count - steps))
    return lax.ppermute(value, axis, [(source, source + steps) for source in range(first, last)])


def face_value(low_side, high_side, in_low, in_high):
    both_in = in_low & in_high
    face_sum = jnp.where(both_in, low_side + high_side, 1.0)
    harmonic = 2.0 * low_side * high_side / face_sum
    return jnp.where(
        both_in,
        harmonic,
        jnp.where(in_low, 2.0 * low_side, jnp.where(in_high, 2.0 * high_side, 0.0)),
    )


def split_weights(low_face, high_face):
    face_sum = low_face + high_face
    safe_sum = jnp.where(face_sum > 0.0, face_sum, 1.0)
    return (low_face / safe_sum, high_face / safe_sum)


def refine(coarse, low_weight, high_weight, along):
    half_count = low_weight.shape[along]
    even_part = lax.slice_in_dim(coarse, 0, half_count, axis=along)
    next_part = lax.slice_in_dim(coarse, 1, half_count + 1, axis=along)
    odd_part = low_weight * even_part + high_weight * next_part
    paired = jnp.stack([even_part, odd_part], axis=along + 1)
    new_shape = list(even_part.shape)
    new_shape[along] = 2 * half_count
    return paired.reshape(new_shape)


def restrict(fine, low_weight, high_weight, along):
    half_count = low_weight.shape[along]
    new_shape = list(fine.shape)
    new_shape[along : along + 1] = [half_count, 2]
    paired = fine.reshape(new_shape)
    even_part = lax.index_in_dim(paired, 0, axis=along + 1, keepdims=False)
    odd_part = lax.index_in_dim(paired, 1, axis=along + 1, keepdims=False)
    pad_after = [(0, 0)] * fine.ndim
    pad_after[along] = (0, 1)
    pad_before = [(0, 0)] * fine.ndim
    pad_before[along] = (1, 0)
    return jnp.pad(even_part + low_weight * odd_part, pad_after) + jnp.pad(
        high_weight * odd_part, pad_before
    )


def prepare(kappa_pad, start_z, start_x, full_z, full_x):
    depth, width, span = kappa_pad.shape
    rows_z = start_z - 1 + jnp.arange(depth, dtype=jnp.int32)
    rows_x = start_x - 1 + jnp.arange(width, dtype=jnp.int32)
    rows_y = jnp.arange(span, dtype=jnp.int32) - 1
    inside = (
        ((rows_z >= 0) & (rows_z < full_z))[:, None, None]
        & ((rows_x >= 0) & (rows_x < full_x))[None, :, None]
        & ((rows_y >= 0) & (rows_y < span - 2))[None, None, :]
    )
    safe_kappa = jnp.where(inside, kappa_pad, 1.0)
    z_faces = face_value(safe_kappa[:-1], safe_kappa[1:], inside[:-1], inside[1:])
    x_faces = face_value(safe_kappa[:, :-1], safe_kappa[:, 1:], inside[:, :-1], inside[:, 1:])
    y_faces = face_value(
        safe_kappa[:, :, :-1], safe_kappa[:, :, 1:], inside[:, :, :-1], inside[:, :, 1:]
    )
    weights_z = split_weights(z_faces[1::2, 1::2, 1::2], z_faces[2::2, 1::2, 1::2])
    weights_y = split_weights(y_faces[1:-1, 1::2, 1::2], y_faces[1:-1, 1::2, 2::2])
    weights_x = split_weights(x_faces[1:-1, 1::2, 1:-1], x_faces[1:-1, 2::2, 1:-1])
    face_z = z_faces[:, 1:-1, 1:-1]
    face_x = x_faces[1:-1, :, 1:-1]
    face_y = y_faces[1:-1, 1:-1, :]
    diagonal = (
        face_z[:-1]
        + face_z[1:]
        + face_x[:, :-1]
        + face_x[:, 1:]
        + face_y[:, :, :-1]
        + face_y[:, :, 1:]
    )
    window_inside = inside[1:-1, 1:-1, 1:-1].astype(jnp.float32)
    return (weights_z, weights_y, weights_x, (face_z, face_x, face_y, diagonal), window_inside)


def refine_probe(colour, setup, start_z, start_x, coarse_z, coarse_x):
    weights_z, weights_y, weights_x, stencil_faces, window_inside = setup
    depth, width, span = window_inside.shape
    level_z = start_z // 2 + jnp.arange(depth // 2 + 1, dtype=jnp.int32)
    level_x = start_x // 2 + jnp.arange(width // 2 + 1, dtype=jnp.int32)
    level_y = jnp.arange(span // 2 + 1, dtype=jnp.int32)
    pick_z = ((level_z % 3 == colour // 9) & (level_z >= 0) & (level_z < coarse_z)).astype(
        jnp.float32
    )
    pick_x = ((level_x % 3 == colour // 3 % 3) & (level_x >= 0) & (level_x < coarse_x)).astype(
        jnp.float32
    )
    pick_y = ((level_y % 3 == colour % 3) & (level_y < span // 2)).astype(jnp.float32)
    probe = pick_z[:, None, None] * pick_x[None, :, None] * pick_y[None, None, :]
    field = refine(probe, weights_z[0], weights_z[1], 0)
    field = refine(field, weights_y[0], weights_y[1], 2)
    field = refine(field, weights_x[0], weights_x[1], 1)
    return field * window_inside


def coarse_image(padded, setup):
    weights_z, weights_y, weights_x, stencil_faces, window_inside = setup
    face_z, face_x, face_y, diagonal = stencil_faces
    center = padded[1:-1, 1:-1, 1:-1]
    image = diagonal * center
    image = image - face_z[:-1] * padded[:-2, 1:-1, 1:-1] - face_z[1:] * padded[2:, 1:-1, 1:-1]
    image = (
        image - face_x[:, :-1] * padded[1:-1, :-2, 1:-1] - face_x[:, 1:] * padded[1:-1, 2:, 1:-1]
    )
    image = (
        image
        - face_y[:, :, :-1] * padded[1:-1, 1:-1, :-2]
        - face_y[:, :, 1:] * padded[1:-1, 1:-1, 2:]
    )
    image = image * window_inside
    coarse = restrict(image, weights_x[0], weights_x[1], 1)
    coarse = restrict(coarse, weights_y[0], weights_y[1], 2)
    coarse = restrict(coarse, weights_z[0], weights_z[1], 0)
    return coarse[:, :, : window_inside.shape[2] // 2]


def assemble(stacked, level_z, level_x, level_y):
    parts = stacked.reshape((3, 3, 3) + stacked.shape[1:])
    offsets = jnp.arange(3, dtype=jnp.int32) - 1
    tones = jnp.arange(3, dtype=jnp.int32)
    match_z = (
        (level_z[None, None, :] + offsets[:, None, None]) % 3 == tones[None, :, None]
    ).astype(jnp.float32)
    match_x = (
        (level_x[None, None, :] + offsets[:, None, None]) % 3 == tones[None, :, None]
    ).astype(jnp.float32)
    match_y = (
        (level_y[None, None, :] + offsets[:, None, None]) % 3 == tones[None, :, None]
    ).astype(jnp.float32)
    first = match_z[:, 0][:, None, None, :, None, None] * parts[0][None]
    for tone in range(1, 3):
        first = first + match_z[:, tone][:, None, None, :, None, None] * parts[tone][None]
    second = match_x[:, 0][None, :, None, None, :, None] * first[:, 0][:, None]
    for tone in range(1, 3):
        second = second + match_x[:, tone][None, :, None, None, :, None] * first[:, tone][:, None]
    third = match_y[:, 0][None, None, :, None, None, :] * second[:, :, 0][:, :, None]
    for tone in range(1, 3):
        third = (
            third + match_y[:, tone][None, None, :, None, None, :] * second[:, :, tone][:, :, None]
        )
    return third.reshape((27,) + stacked.shape[1:])


def per_device(material, diffusivity, variation):
    depth, width, span = material.shape
    base = jnp.zeros(material.shape, jnp.float32)
    for which in range(NMAT):
        base = base + jnp.where(material == which, diffusivity[which], 0.0)
    kappa = base * variation
    full_z = depth * lax.axis_size("gz")
    full_x = width * lax.axis_size("xy")
    block_z = lax.axis_index("gz") * depth
    block_x = lax.axis_index("xy") * width
    colours = jnp.arange(27, dtype=jnp.int32)
    bordered = with_halo(kappa, (("xy", 1), ("gz", 0)), 1)
    kappa_pad = jnp.pad(bordered, ((0, 0), (0, 0), (1, 1)))
    setup = prepare(kappa_pad, block_z, block_x, full_z, full_x)

    def make_probe(colour):
        return refine_probe(colour, setup, block_z, block_x, full_z // 2, full_x // 2)

    probes = lax.map(make_probe, colours)
    framed = with_halo(probes, (("xy", 2), ("gz", 1)), 1)
    padded_all = jnp.pad(framed, ((0, 0), (0, 0), (0, 0), (1, 1)))

    def image_of(padded):
        return coarse_image(padded, setup)

    images = lax.map(image_of, padded_all)
    top_plane = images[:, depth // 2]
    arrived = passed_along(top_plane, "gz", 1)
    images = images[:, : depth // 2]
    images = images.at[:, 0].add(arrived)
    side_column = images[:, :, width // 2]
    landed = passed_along(side_column, "xy", 1)
    stacked = images[:, :, : width // 2].at[:, :, 0].add(landed)
    level_z = block_z // 2 + jnp.arange(depth // 2, dtype=jnp.int32)
    level_x = block_x // 2 + jnp.arange(width // 2, dtype=jnp.int32)
    level_y = jnp.arange(span // 2, dtype=jnp.int32)
    return assemble(stacked, level_z, level_x, level_y)


def solution(mesh):
    placed = (P("gz", "xy", None), P(), P("gz", "xy", None))
    return jax.shard_map(
        per_device, mesh=mesh, in_specs=placed, out_specs=P(None, "gz", "xy", None), check_vma=False
    )
```

profile of v0, /device:TPU:34, one launch (start us, length us, event | category | flops | bytes accessed | tf_op | source)
XLA Modules:
  0.0 329.0 jit_solution(17918605530401027331)
XLA Ops:
  0.0 1.6 fusion.50
  1.6 5.9 %copy_multiply_fusion = f32[4,16,256]{2,0,1:T(4,128)S(1)} fusion(f32[4,16,256]{2,1,0:T(8,128)} %param.13, s32[4,16,256]{2,1,0:T(8,128)} %param.11, f32[]{:T(128)} %bitcast.34, f32[]{:T(128)} %bitcast.33, f32[]{:T(128)} %bitcast.32, f32[]{:T(128)} %bitcast.31, f32[]{:T(128)} %bitcast.30, f32[]{:T(128)} %bitcast.29, f32[]{:T(128)} %bitcast.28, f32[]{:T(128)} %bitcast.27), kind=kLoop, calls=%fused_computation.92 | loop fusion | flops 393216 | bytes 196640 | tf_op jit(solution)/shard_map/mul | solution.py:179
  7.6 1.9 collective-permute-start
  9.5 10.3 %collective-permute-start.1 = (f32[4,1,256]{2,0,1:T(4,128)S(1)}, f32[4,1,256]{2,0,1:T(4,128)S(1)}, u32[]{:S(2)}, u32[]{:S(2)}) collective-permute-start(f32[4,1,256]{2,0,1:T(4,128)S(1)} %get-tuple-element.750), channel_id=1, source_target_pairs={{4,0},{8,4},{12,8},{16,12},{20,16},{24,20},{28,24},{32,28},{36,32}... | collective-permute-start | bytes 12296 | tf_op jit(solution)/shard_map/ppermute | solution.py:17
  21.1 3.4 %collective-permute-start.2 = (f32[1,18,256]{2,0,1:T(1,128)S(1)}, f32[1,18,256]{2,0,1:T(1,128)S(1)}, u32[]{:S(2)}, u32[]{:S(2)}) collective-permute-start(f32[1,18,256]{2,0,1:T(1,128)S(1)} %get-tuple-element.747), channel_id=1, source_target_pairs={{0,1},{1,2},{2,3},{4,5},{5,6},{6,7},{8,9},{9,10},{10,11},{12,13},{... | collective-permute-start | bytes 55304 | tf_op jit(solution)/shard_map/ppermute | solution.py:14
  24.5 2.4 collective-permute-start.3
  27.6 2.6 collective-permute-done.3
  30.7 2.1 slice.450
  32.8 2.1 slice.451
  35.0 2.1 slice.444
  37.1 2.1 slice.445
  39.9 165.8 %while.27 = (s32[]{:T(128)}, f32[27,4,16,256]{3,1,2,0:T(4,128)}, s32[]{:T(128)}, s32[27]{0:T(128)S(1)}, s32[]{:T(128)}, /*index=5*/f32[2,9,129]{2,0,1:T(2,128)S(...) while((s32[]{:T(128)}, f32[27,4,16,256]{3,1,2,0:T(4,128)}, ...), condition=%wide.region_1.2_spmd, body=%wide.region_0.1_spmd.sunk | while | flops 96976 | bytes 1096827 | solution.py:192
  205.8 1.0 fusion.47
  206.8 1.9 collective-permute-start.4
  208.7 7.0 %collective-permute-start.5 = (f32[27,4,1,256]{3,1,2,0:T(4,128)S(1)}, f32[27,4,1,256]{3,1,2,0:T(4,128)S(1)}, u32[]{:S(2)}, u32[]{:S(2)}) collective-permute-start(f32[27,4,1,256]{3,1,2,0:T(4,128)S(1)} %get-tuple-element.734), channel_id=1, source_target_pairs={{4,0},{8,4},{12,8},{16,12},{20,16},{24,20},{28,24},{32,28},{36,32}... | collective-permute-start | bytes 331784 | tf_op jit(solution)/shard_map/ppermute | solution.py:17
  216.2 2.0 constant_dynamic-update-slice_fusion.1
  218.3 1.7 fusion.46
  220.0 3.1 collective-permute-start.6
  223.1 3.5 %collective-permute-start.7 = (f32[27,1,18,256]{3,1,2,0:T(1,128)}, f32[27,1,18,256]{3,1,2,0:T(1,128)}, u32[]{:S(2)}, u32[]{:S(2)}) collective-permute-start(f32[27,1,18,256]{3,1,2,0:T(1,128)} %get-tuple-element.733), channel_id=1, source_target_pairs={{1,0},{2,1},{3,2},{5,4},{6,5},{7,6},{9,8},{10,9},{11,10},{13,12},{... | collective-permute-start | bytes 1493000 | tf_op jit(solution)/shard_map/ppermute | solution.py:17
  228.3 1.0 slice.540
  229.3 1.2 slice_add_fusion.1
  231.1 3.1 collective-permute-done.7
  234.2 8.1 %select_maximum_fusion = f32[27,6,18,258]{3,1,2,0:T(8,128)} fusion(f32[27,1,18,256]{3,1,2,0:T(1,128)} %collective-permute-done.7, f32[27,4,18,256]{3,1,2,0:T(4,128)S(1)} %constant_dynamic-update-slice_fusion, f32[27,1,18,256]{3,1,2,0:T(1,128)} %collective-permute-done.6), kind=kLoop, calls=%fused_computation.55 | loop fusion | flops 6018624 | bytes 5995296 | tf_op jit(solution)/shard_map/concatenate | solution.py:18
  242.3 65.8 %while.28 = (s32[]{:T(128)}, f32[27,3,9,128]{3,1,2,0:T(4,128)S(1)}, f32[27,6,18,258]{3,1,2,0:T(8,128)}, f32[4,16,256]{2,0,1:T(4,128)S(1)}, f32[5,16,256]{2,0,1:T...) while((s32[]{:T(128)}, f32[27,3,9,128]{3,1,2,0:T(4,128)S(1)}, ...), condition=%wide.region_3.4_spmd, body=%wide.region_2.3_spmd.sunk | while | flops 292060 | bytes 2069461 | solution.py:199
  244.8 1.0 dynamic-slice_bitcast_fusion.2
  247.2 1.0 dynamic-slice_bitcast_fusion.2
  254.5 1.0 dynamic-slice_bitcast_fusion.2
  308.2 1.9 collective-permute-start.8
  310.3 5.0 %collective-permute-done.8 = f32[27,9,128]{2,0,1:T(8,128)S(1)} collective-permute-done((f32[27,9,128]{2,0,1:T(8,128)S(1)}, f32[27,9,128]{2,0,1:T(8,128)S(1)}, u32[]{:S(2)}, u32[]{:S(2)}) %collective-permute-start.8) | collective-permute-done | bytes 124448 | tf_op jit(solution)/shard_map/ppermute | solution.py:25
  315.4 3.8 %scatter-add.6 = f32[27,2,9,128]{3,1,2,0:T(2,128)S(1)} dynamic-update-slice(f32[27,2,9,128]{3,1,2,0:T(2,128)S(1)} %slice.472, f32[27,1,9,128]{3,1,2,0:T(1,128)S(1)} %copy.227, s32[]{:T(128)} %constant.290.clone.1, s32[]{:T(128)} %constant.290.clone.1, s32[]{:T(128)} %constant.290.clone.1, s32[]{:T(128)} %constant.290.clone.1) | dynamic-update-slice | bytes 248836 | tf_op jit(solution)/shard_map/scatter-add | solution.py:203
  319.3 1.9 collective-permute-start.9
  321.6 6.2 %collective-permute-done.9 = f32[27,2,128]{2,1,0:T(2,128)S(1)} collective-permute-done((f32[27,2,128]{2,1,0:T(2,128)S(1)}, f32[27,2,128]{2,1,0:T(2,128)S(1)}, u32[]{:S(2)}, u32[]{:S(2)}) %collective-permute-start.9) | collective-permute-done | bytes 27680 | tf_op jit(solution)/shard_map/ppermute | solution.py:25
  (907 shorter events, 137.5 us)
Async XLA Ops:
  7.6 13.4 %collective-permute-start = (f32[4,1,256]{2,0,1:T(4,128)S(1)}, f32[4,1,256]{2,0,1:T(4,128)S(1)}, u32[]{:S(2)}, u32[]{:S(2)}) collective-permute-start(f32[4,1,256]{2,0,1:T(4,128)S(1)} %get-tuple-element.749), channel_id=1, source_target_pairs={{0,4},{4,8},{8,12},{12,16},{16,20},{20,24},{24,28},{28,32},{32,36}... | collective-permute-start | bytes 12296 | tf_op jit(solution)/shard_map/ppermute | solution.py:14
  9.5 11.6 %collective-permute-start.1 = (f32[4,1,256]{2,0,1:T(4,128)S(1)}, f32[4,1,256]{2,0,1:T(4,128)S(1)}, u32[]{:S(2)}, u32[]{:S(2)}) collective-permute-start(f32[4,1,256]{2,0,1:T(4,128)S(1)} %get-tuple-element.750), channel_id=1, source_target_pairs={{4,0},{8,4},{12,8},{16,12},{20,16},{24,20},{28,24},{32,28},{36,32}... | collective-permute-start | bytes 12296 | tf_op jit(solution)/shard_map/ppermute | solution.py:17
  19.8 1.1 copy-start.12
  21.1 6.5 %collective-permute-start.2 = (f32[1,18,256]{2,0,1:T(1,128)S(1)}, f32[1,18,256]{2,0,1:T(1,128)S(1)}, u32[]{:S(2)}, u32[]{:S(2)}) collective-permute-start(f32[1,18,256]{2,0,1:T(1,128)S(1)} %get-tuple-element.747), channel_id=1, source_target_pairs={{0,1},{1,2},{2,3},{4,5},{5,6},{6,7},{8,9},{9,10},{10,11},{12,13},{... | collective-permute-start | bytes 55304 | tf_op jit(solution)/shard_map/ppermute | solution.py:14
  24.5 5.7 %collective-permute-start.3 = (f32[1,18,256]{2,0,1:T(1,128)S(1)}, f32[1,18,256]{2,0,1:T(1,128)S(1)}, u32[]{:S(2)}, u32[]{:S(2)}) collective-permute-start(f32[1,18,256]{2,0,1:T(1,128)S(1)} %get-tuple-element.748), channel_id=1, source_target_pairs={{1,0},{2,1},{3,2},{5,4},{6,5},{7,6},{9,8},{10,9},{11,10},{13,12},{... | collective-permute-start | bytes 55304 | tf_op jit(solution)/shard_map/ppermute | solution.py:17
  30.7 2.1 copy-start.1
  205.8 9.9 %copy-start.2 = (f32[4,9,128]{2,0,1:T(4,128)}, f32[4,9,128]{2,0,1:T(4,128)S(1)}, u32[]{:S(2)}) copy-start(f32[4,9,128]{2,0,1:T(4,128)S(1)} %get-tuple-element.1070) | copy-start | bytes 55300
  205.8 9.9 %copy-start.4 = (f32[4,9,128]{2,0,1:T(4,128)}, f32[4,9,128]{2,0,1:T(4,128)S(1)}, u32[]{:S(2)}) copy-start(f32[4,9,128]{2,0,1:T(4,128)S(1)} %get-tuple-element.1071) | copy-start | bytes 55300
  206.8 9.4 %collective-permute-start.4 = (f32[27,4,1,256]{3,1,2,0:T(4,128)S(1)}, f32[27,4,1,256]{3,1,2,0:T(4,128)S(1)}, u32[]{:S(2)}, u32[]{:S(2)}) collective-permute-start(f32[27,4,1,256]{3,1,2,0:T(4,128)S(1)} %get-tuple-element.735), channel_id=1, source_target_pairs={{0,4},{4,8},{8,12},{12,16},{16,20},{20,24},{24,28},{28,32},{32,36}... | collective-permute-start | bytes 331784 | tf_op jit(solution)/shard_map/ppermute | solution.py:14
  208.7 9.6 %collective-permute-start.5 = (f32[27,4,1,256]{3,1,2,0:T(4,128)S(1)}, f32[27,4,1,256]{3,1,2,0:T(4,128)S(1)}, u32[]{:S(2)}, u32[]{:S(2)}) collective-permute-start(f32[27,4,1,256]{3,1,2,0:T(4,128)S(1)} %get-tuple-element.734), channel_id=1, source_target_pairs={{4,0},{8,4},{12,8},{16,12},{20,16},{24,20},{28,24},{32,28},{36,32}... | collective-permute-start | bytes 331784 | tf_op jit(solution)/shard_map/ppermute | solution.py:17
  218.2 8.4 %copy-start.13 = (s32[3]{0:T(128)S(1)}, s32[3]{0:T(128)}, u32[]{:S(2)}) copy-start(s32[3]{0:T(128)} %copy-done.12) | copy-start | bytes 40
  218.2 9.0 %copy-start.6 = (f32[3,3,128]{2,0,1:T(4,128)S(1)}, f32[3,3,128]{2,0,1:T(4,128)}, u32[]{:S(2)}) copy-start(f32[3,3,128]{2,0,1:T(4,128)} %fusion.33) | copy-start | bytes 13828
  218.2 9.6 %copy-start.5 = (f32[4,9,128]{2,0,1:T(4,128)S(1)}, f32[4,9,128]{2,0,1:T(4,128)}, u32[]{:S(2)}) copy-start(f32[4,9,128]{2,0,1:T(4,128)} %copy-done.4) | copy-start | bytes 55300
  218.2 9.8 %copy-start.3 = (f32[4,9,128]{2,0,1:T(4,128)S(1)}, f32[4,9,128]{2,0,1:T(4,128)}, u32[]{:S(2)}) copy-start(f32[4,9,128]{2,0,1:T(4,128)} %copy-done.2) | copy-start | bytes 55300
  220.0 11.1 %collective-permute-start.6 = (f32[27,1,18,256]{3,1,2,0:T(1,128)}, f32[27,1,18,256]{3,1,2,0:T(1,128)}, u32[]{:S(2)}, u32[]{:S(2)}) collective-permute-start(f32[27,1,18,256]{3,1,2,0:T(1,128)} %get-tuple-element.732), channel_id=1, source_target_pairs={{0,1},{1,2},{2,3},{4,5},{5,6},{6,7},{8,9},{9,10},{10,11},{12,13},{... | collective-permute-start | bytes 1493000 | tf_op jit(solution)/shard_map/ppermute | solution.py:14
  223.1 11.1 %collective-permute-start.7 = (f32[27,1,18,256]{3,1,2,0:T(1,128)}, f32[27,1,18,256]{3,1,2,0:T(1,128)}, u32[]{:S(2)}, u32[]{:S(2)}) collective-permute-start(f32[27,1,18,256]{3,1,2,0:T(1,128)} %get-tuple-element.733), channel_id=1, source_target_pairs={{1,0},{2,1},{3,2},{5,4},{6,5},{7,6},{9,8},{10,9},{11,10},{13,12},{... | collective-permute-start | bytes 1493000 | tf_op jit(solution)/shard_map/ppermute | solution.py:17
  230.6 11.8 %copy-start = (f32[27,3,9,128]{3,1,2,0:T(4,128)S(1)}, f32[27,3,9,128]{3,1,2,0:T(4,128)}, u32[]{:S(2)}) copy-start(f32[27,3,9,128]{3,1,2,0:T(4,128)} %custom-call.2) | copy-start | bytes 1119748
  242.3 67.8 %copy-start.14 = (s32[3,2]{0,1:T(2,128)S(1)}, s32[3,2]{0,1:T(2,128)}, u32[]{:S(2)}) copy-start(s32[3,2]{0,1:T(2,128)} %and_select_fusion.3) | copy-start | bytes 76
  308.1 13.4 %copy-start.11 = (f32[3,128]{1,0:T(4,128)S(1)}, f32[3,128]{1,0:T(4,128)}, u32[]{:S(2)}) copy-start(f32[3,128]{1,0:T(4,128)} %get-tuple-element.755) | copy-start | bytes 4612
  308.1 13.4 %copy-start.10 = (f32[3,128]{1,0:T(4,128)S(1)}, f32[3,128]{1,0:T(4,128)}, u32[]{:S(2)}) copy-start(f32[3,128]{1,0:T(4,128)} %get-tuple-element.757) | copy-start | bytes 4612
  308.2 13.4 %copy-start.9 = (f32[3,128]{1,0:T(4,128)S(1)}, f32[3,128]{1,0:T(4,128)}, u32[]{:S(2)}) copy-start(f32[3,128]{1,0:T(4,128)} %get-tuple-element.756) | copy-start | bytes 4612
  308.2 7.0 %collective-permute-start.8 = (f32[27,9,128]{2,0,1:T(8,128)S(1)}, f32[27,9,128]{2,0,1:T(8,128)S(1)}, u32[]{:S(2)}, u32[]{:S(2)}) collective-permute-start(f32[27,9,128]{2,0,1:T(8,128)S(1)} %slice_bitcast_fusion.5), channel_id=1, source_target_pairs={{0,1},{1,2},{2,3},{4,5},{5,6},{6,7},{8,9},{9,10},{10,11},{12,13},{... | collective-permute-start | bytes 373256 | tf_op jit(solution)/shard_map/ppermute | solution.py:25
  310.2 17.9 %copy-start.7 = (f32[3,8]{1,0:T(4,128)S(1)}, f32[3,8]{1,0:T(4,128)}, u32[]{:S(2)}) copy-start(f32[3,8]{1,0:T(4,128)} %get-tuple-element.759) | copy-start | bytes 292
  310.2 17.9 %copy-start.8 = (f32[3,8]{1,0:T(4,128)S(1)}, f32[3,8]{1,0:T(4,128)}, u32[]{:S(2)}) copy-start(f32[3,8]{1,0:T(4,128)} %get-tuple-element.760) | copy-start | bytes 292
  319.3 8.5 %collective-permute-start.9 = (f32[27,2,128]{2,1,0:T(2,128)S(1)}, f32[27,2,128]{2,1,0:T(2,128)S(1)}, u32[]{:S(2)}, u32[]{:S(2)}) collective-permute-start(f32[27,2,128]{2,1,0:T(2,128)S(1)} %slice_bitcast_fusion.12), channel_id=1, source_target_pairs={{0,4},{4,8},{8,12},{12,16},{16,20},{20,24},{24,28},{28,32},{32,36}... | collective-permute-start | bytes 82952 | tf_op jit(solution)/shard_map/ppermute | solution.py:25
where the time goes:
time: 332 us; the launch traced here: 329 us
  local copies, waits for them, and re-layouts  106 us (32%)
  loops' own time  98.8 us (30%)
  other arithmetic  67.8 us (20%)
  starting transfers between devices  37.4 us (11%)
  waiting for transfers between devices  18 us (5%)
    another operation x1, loops' own time, per_device(): probes = lax.map(make_probe, colours)  96.5 us
    squeeze x27, local copies, waits for them, and re-layouts, per_device(): images = lax.map(image_of, padded_all)  25.8 us
    ppermute x4, starting transfers between devices, with_halo(): lax.ppermute(lax.slice_in_dim(block, 0, width, axis=dim), axis, backward)  23.2 us
    dynamic_update_slice x27, other arithmetic, per_device(): probes = lax.map(make_probe, colours)  18.1 us
    dynamic_slice x27, local copies, waits for them, and re-layouts, per_device(): probes = lax.map(make_probe, colours)  17.8 us
    another operation x81, local copies, waits for them, and re-layouts, refine(): paired = jnp.stack([even_part, odd_part], axis=along + 1)  15.7 us
    another operation x162, other arithmetic, refine(): paired = jnp.stack([even_part, odd_part], axis=along + 1)  11.8 us
    slice x54, local copies, waits for them, and re-layouts, restrict(): even_part = lax.index_in_dim(paired, 0, axis=along + 1, keepdims=False)  11.5 us
  transfers between devices with their start and end apart: 10, of which 7 were waited for; matrix products, arithmetic and copies ran while one was open for 2% of the time, Pallas kernels for 0%

commit v1 on v0

v1 whole, which is shorter than its diff:
```python
import functools

import jax
import jax.numpy as jnp
from jax import lax
from jax.experimental import pallas as pl
from jax.experimental.pallas import tpu as pltpu
from jax.sharding import PartitionSpec as P

MESH = pl.DeviceIdType.MESH
OUTSIDE = -1e-18
STEPS = [(dz, dx) for dz in (-1, 0, 1) for dx in (-1, 0, 1) if (dz, dx) != (0, 0)]


class Rows:
    def __init__(self, own, edge):
        self.own, self.edge = own, edge

    def __add__(self, other):
        return Rows(self.own + other.own, self.edge + other.edge)

    def __mul__(self, other):
        return Rows(self.own * other.own, self.edge * other.edge)

    def map(self, function):
        return Rows(function(self.own), function(self.edge))


def row_index():
    return lax.broadcasted_iota(jnp.int32, (8, 128), 0)


def lane_index():
    return lax.broadcasted_iota(jnp.int32, (8, 128), 1)


def next_row(value):
    last = row_index() == 7
    own = pltpu.roll(value.own, 7, 0)
    edge = pltpu.roll(value.edge, 7, 0)
    return Rows(jnp.where(last, edge, own), jnp.where(last, own, edge))


def previous_row(value):
    first = row_index() == 0
    return jnp.where(first, pltpu.roll(value.edge, 1, 0), pltpu.roll(value.own, 1, 0))


def next_lane(value):
    return pltpu.roll(value, 127, 1)


def previous_lane(value):
    return pltpu.roll(value, 1, 1)


def next_lane_bounded(value):
    return jnp.where(lane_index() == 127, OUTSIDE, next_lane(value))


def previous_lane_bounded(value):
    return jnp.where(lane_index() == 0, OUTSIDE, previous_lane(value))


def without_last(value):
    return jnp.where(lane_index() == 127, 0.0, value)


def inverse(value):
    return 1.0 / value


class Plane:
    pass


def weights_of(load):
    plane = Plane()
    plane.rho = [[load(xp, yp) for yp in (0, 1)] for xp in (0, 1)]
    plane.low, plane.high, plane.link = [], [], []
    for yp in (0, 1):
        even, odd = plane.rho[0][yp], plane.rho[1][yp]
        before = even + odd
        after = odd + next_row(even)
        link = (before + after).map(inverse)
        plane.low.append(after * link)
        plane.high.append(before * link)
        plane.link.append(link)
    even, odd = plane.rho[0]
    plane.before = even + odd
    plane.after = odd + even.map(next_lane_bounded)
    scale = (plane.before + plane.after).map(inverse)
    plane.y_low = plane.after * scale
    plane.y_high = (plane.before * scale).map(without_last)
    plane.y_low_next = next_row(plane.y_low)
    plane.y_high_next = next_row(plane.y_high)
    return plane


def z_link(lower, upper):
    steps = []
    faces = []
    for yp in (0, 1):
        even = inverse(lower.rho[0][yp].own + upper.rho[0][yp].own)
        odd = (lower.rho[1][yp] + upper.rho[1][yp]).map(inverse)
        low, high = lower.low[yp] * odd, lower.high[yp] * odd
        same = even + (low * upper.low[yp]).own + previous_row(high * upper.high[yp])
        steps.append((same, low * upper.high[yp], high * upper.low[yp]))
        faces.append((even, odd))
    (even_same, even_up, even_down), (odd_same, odd_up, odd_down) = steps
    z = Plane()
    z.faces = faces
    first, second = lower.y_low.own * odd_same, lower.y_high.own * odd_same
    z.same = (
        even_same + first * upper.y_low.own + previous_lane(second * upper.y_high.own),
        first * upper.y_high.own,
        second * upper.y_low.own,
    )
    first, second = lower.y_low * odd_up, lower.y_high * odd_up
    z.up = (
        even_up + first * upper.y_low_next + (second * upper.y_high_next).map(previous_lane),
        first * upper.y_high_next,
        second * upper.y_low_next,
    )
    first, second = lower.y_low_next * odd_down, lower.y_high_next * odd_down
    z.down = (
        even_down + first * upper.y_low + (second * upper.y_high).map(previous_lane),
        first * upper.y_high,
        second * upper.y_low,
    )
    return z


def within(plane, faces_below, faces_above):
    even_before = inverse(plane.before.own)
    even_after = inverse(plane.after.own)
    (odd_e, odd_o) = plane.rho[1]
    odd_before = (odd_e + odd_o).map(inverse)
    odd_after = (odd_o + odd_e.map(next_lane_bounded)).map(inverse)

    def lower_face(face, rho):
        return jnp.where(lane_index() == 0, inverse(rho), previous_lane(face))

    even_lower = lower_face(even_after, plane.rho[0][0].own + OUTSIDE)
    odd_lower = Rows(
        lower_face(odd_after.own, odd_e.own + OUTSIDE),
        lower_face(odd_after.edge, odd_e.edge + OUTSIDE),
    )
    even_sum = [
        even_before + even_lower + faces_below[0][0] + faces_above[0][0],
        even_before + even_after + faces_below[1][0] + faces_above[1][0],
    ]
    odd_sum = [
        odd_before + odd_lower + faces_below[0][1] + faces_above[0][1],
        odd_before + odd_after + faces_below[1][1] + faces_above[1][1],
    ]
    centre, along = [], []
    for yp in (0, 1):
        low, high, link = plane.low[yp], plane.high[yp], plane.link[yp]
        low_sum, high_sum = low * odd_sum[yp], high * odd_sum[yp]
        centre.append(
            even_sum[yp]
            + (link + low_sum * low).own
            + previous_row(link + high_sum * high)
        )
        along.append(
            Rows(
                link.own - low_sum.own * high.own,
                link.edge - low_sum.edge * high.edge,
            )
        )
    even_after = without_last(even_after)
    odd_after = odd_after.map(without_last)
    low_e, low_o = plane.low
    high_e, high_o = plane.high
    low_n, high_n = low_e.map(next_lane), high_e.map(next_lane)
    first, second = low_o * odd_before, high_o * odd_before
    before = (
        even_before + (first * low_e).own + previous_row(second * high_e),
        second * low_e,
        first * high_e,
    )
    first, second = low_o * odd_after, high_o * odd_after
    after = (
        even_after + (first * low_n).own + previous_row(second * high_n),
        first * high_n,
        second * low_n,
    )
    low, high = plane.y_low, plane.y_high
    low_next, high_next = plane.y_low_next, plane.y_high_next
    c = Plane()
    cross = low.own * centre[1]
    c.side = high.own * before[0] + low.own * after[0] - cross * high.own
    c.centre = (
        centre[0]
        + low.own * (cross - before[0] - before[0])
        + previous_lane(high.own * (high.own * centre[1] - after[0] - after[0]))
    )
    one = low * along[1] + before[1]
    two = high * along[1] + after[2]
    c.up = (
        along[0]
        + low_next * one
        + low * before[2]
        + (high_next * two + high * after[1]).map(previous_lane),
        high_next * one + low * after[1],
        low_next * two + high * before[2],
    )
    return c


def z_weights(below, middle, above):
    before = below.rho[0][0] + middle.rho[0][0]
    after = middle.rho[0][0] + above.rho[0][0]
    scale = (before + after).map(inverse)

    def versions(value):
        lane = value.map(next_lane)
        row = next_row(value)
        return (value, lane, row, row.map(next_lane))

    return versions(after * scale), versions(before * scale)


def between(weights, inner, low_link, high_link):
    (lo, lo_j, lo_i, lo_ij), (hi, hi_j, hi_i, hi_ij) = weights

    def term(first, second, low, high, own):
        return second * (low + first * own) + first * high

    same = (
        hi.own * (low_link.same[0] - lo.own * inner.centre) + lo.own * high_link.same[0],
        term(lo.own, hi_j.own, low_link.same[1], high_link.same[1], inner.side),
        term(lo_j.own, hi.own, low_link.same[2], high_link.same[2], inner.side),
    )
    up = (
        term(lo, hi_i, low_link.up[0], high_link.up[0], inner.up[0]),
        term(lo, hi_ij, low_link.up[1], high_link.up[1], inner.up[1]),
        term(lo_j, hi_i, low_link.up[2], high_link.up[2], inner.up[2]),
    )
    down = (
        term(lo_i, hi, low_link.down[0], high_link.down[0], inner.up[0]),
        term(lo_i, hi_j, low_link.down[1], high_link.down[1], inner.up[2]),
        term(lo_ij, hi, low_link.down[2], high_link.down[2], inner.up[1]),
    )
    return same, up, down


def level(own, below, above):
    centre, side = own.centre, own.side
    up = list(own.up)
    (_, hi), inner, link = below
    hi, hi_j, hi_i, hi_ij = hi
    centre = centre + hi.own * (hi.own * inner.centre - link.same[0] - link.same[0])
    side = side + hi.own * (hi_j.own * inner.side + link.same[1]) + hi_j.own * link.same[2]
    up[0] = up[0] + hi * (hi_i * inner.up[0] + link.up[0]) + hi_i * link.down[0]
    up[1] = up[1] + hi * (hi_ij * inner.up[1] + link.up[1]) + hi_ij * link.down[2]
    up[2] = up[2] + hi_j * (hi_i * inner.up[2] + link.up[2]) + hi_i * link.down[1]
    (lo, _), inner, link = above
    lo, lo_j, lo_i, lo_ij = lo
    centre = centre + lo.own * (lo.own * inner.centre - link.same[0] - link.same[0])
    side = side + lo_j.own * (lo.own * inner.side + link.same[1]) + lo.own * link.same[2]
    up[0] = up[0] + lo_i * (lo * inner.up[0] + link.up[0]) + lo * link.down[0]
    up[1] = up[1] + lo_ij * (lo * inner.up[1] + link.up[1]) + lo * link.down[2]
    up[2] = up[2] + lo_i * (lo_j * inner.up[2] + link.up[2]) + lo_j * link.down[1]
    return centre, side, up


def stencil_of(load, store):
    planes = [weights_of(functools.partial(load, p)) for p in range(7)]
    links = [z_link(planes[p], planes[p + 1]) for p in range(6)]
    inner = [None] * 7
    for p in range(1, 6):
        inner[p] = within(planes[p], links[p - 1].faces, links[p].faces)
    weights = [None] * 7
    for p in (1, 3, 5):
        weights[p] = z_weights(planes[p - 1], planes[p], planes[p + 1])
    for p in (1, 3, 5):
        same, up, down = between(weights[p], inner[p], links[p - 1], links[p])
        plane = (p - 1) // 2
        if plane < 2:
            low = functools.partial(store, -1)
            low(0, 0, plane, same[0])
            low(0, 1, plane, same[2])
            low(0, -1, plane, previous_lane(same[1]))
            low(1, 0, plane, down[0].own)
            low(1, 1, plane, down[2].own)
            low(1, -1, plane, previous_lane(down[1].own))
            low(-1, 0, plane, previous_row(up[0]))
            low(-1, 1, plane, previous_row(up[2]))
            low(-1, -1, plane, previous_lane(previous_row(up[1])))
        if plane > 0:
            high = functools.partial(store, 1)
            high(0, 0, plane - 1, same[0])
            high(0, 1, plane - 1, same[1])
            high(0, -1, plane - 1, previous_lane(same[2]))
            high(1, 0, plane - 1, up[0].own)
            high(1, 1, plane - 1, up[1].own)
            high(1, -1, plane - 1, previous_lane(up[2].own))
            high(-1, 0, plane - 1, previous_row(down[0]))
            high(-1, 1, plane - 1, previous_row(down[1]))
            high(-1, -1, plane - 1, previous_lane(previous_row(down[2])))
    for plane in (0, 1):
        p = 2 * plane + 2
        centre, side, up = level(
            inner[p],
            (weights[p - 1], inner[p - 1], links[p - 1]),
            (weights[p + 1], inner[p + 1], links[p]),
        )
        here = functools.partial(store, 0)
        here(0, 0, plane, -centre)
        here(0, 1, plane, side)
        here(0, -1, plane, previous_lane(side))
        here(1, 0, plane, up[0].own)
        here(-1, 0, plane, previous_row(up[0]))
        here(1, 1, plane, up[1].own)
        here(-1, -1, plane, previous_lane(previous_row(up[1])))
        here(1, -1, plane, previous_lane(up[2].own))
        here(-1, 1, plane, previous_row(up[2]))


def split_lanes(value):
    lane = lax.broadcasted_iota(jnp.int32, (16, 128), 1)
    left, right = value[:, :128], value[:, 128:]
    first = (lane * 2) % 128 + lane // 64
    left = jnp.take_along_axis(left, first, axis=1)
    right = jnp.take_along_axis(right, (first + 1) % 2 + first // 2 * 2, axis=1)
    even = jnp.where(lane < 64, left, right)
    odd = pltpu.roll(jnp.where(lane < 64, right, left), 64, 1)
    return even, odd


def exchange_kernel(material, diffusivity, variation, out, split, send_sem, recv_sem):
    gz, xy = lax.axis_index("gz"), lax.axis_index("xy")
    count_z, count_x = lax.axis_size("gz"), lax.axis_size("xy")

    def device(dz, dx):
        return {
            "gz": lax.rem(gz + (dz + count_z), count_z),
            "xy": lax.rem(xy + (dx + count_x), count_x),
        }

    barrier = pltpu.get_barrier_semaphore()
    for dz, dx in STEPS:
        pl.semaphore_signal(barrier, inc=1, device_id=device(dz, dx), device_id_type=MESH)

    table = [diffusivity[which] for which in range(8)]
    for k in range(4):
        which = material[k]
        bits = [(which & bit) != 0 for bit in (1, 2, 4)]
        values = table
        for bit in bits:
            values = [
                jnp.where(bit, values[2 * n + 1], values[2 * n])
                for n in range(len(values) // 2)
            ]
        rho = -0.5 / (values[0] * variation[k])
        for yp, half in enumerate(split_lanes(rho)):
            split[k, yp] = half
            for xp in (0, 1):
                out[0, k + 2, xp, yp] = split[k, yp, pl.ds(xp, 8, stride=2), :]

    pl.semaphore_wait(barrier, len(STEPS))
    copies = []
    for n, (dz, dx) in enumerate(STEPS):
        source = {-1: pl.ds(2, 1), 0: pl.ds(2, 4), 1: pl.ds(4, 2)}[dz]
        target = {-1: pl.ds(6, 1), 0: pl.ds(2, 4), 1: pl.ds(0, 2)}[dz]
        if dx == 0:
            src, dst = out.at[0, source], out.at[0, target]
        elif dx == 1:
            rows = (slice(None), slice(None), pl.ds(7, 1))
            src, dst = out.at[(0, source) + rows], out.at[(1, target) + rows]
        else:
            rows = (0, slice(None), pl.ds(0, 1))
            src, dst = out.at[(0, source) + rows], out.at[(1, target) + rows]
        copy = pltpu.make_async_remote_copy(
            src_ref=src,
            dst_ref=dst,
            send_sem=send_sem.at[n],
            recv_sem=recv_sem.at[n],
            device_id=device(dz, dx),
            device_id_type=MESH,
        )
        copy.start()
        copies.append(copy)
    for copy in copies:
        copy.wait()

    @pl.when(gz == 0)
    def _():
        out[:, 0:2] = jnp.full((2, 2, 2, 2, 8, 128), OUTSIDE, jnp.float32)

    @pl.when(gz == count_z - 1)
    def _():
        out[:, 6] = jnp.full((2, 2, 2, 8, 128), OUTSIDE, jnp.float32)

    @pl.when(xy == 0)
    def _():
        out[1, :, :, :, 7, :] = jnp.full((7, 2, 2, 128), OUTSIDE, jnp.float32)

    @pl.when(xy == count_x - 1)
    def _():
        out[1, :, 0, :, 0, :] = jnp.full((7, 2, 128), OUTSIDE, jnp.float32)


def stencil_kernel(rho, out):
    gz, xy = lax.axis_index("gz"), lax.axis_index("xy")

    def load(p, xp, yp):
        return Rows(rho[0, p, xp, yp], rho[1, p, xp, yp])

    def store(dz, dx, dy, plane, value):
        out[9 * (dz + 1) + 3 * (dx + 1) + dy + 1, plane] = value

    stencil_of(load, store)
    nothing = jnp.zeros((1, 128), jnp.float32)

    def clear_row(dx, row):
        for dz in (-1, 0, 1):
            for dy in (-1, 0, 1):
                for plane in (0, 1):
                    entry = 9 * (dz + 1) + 3 * (dx + 1) + dy + 1
                    out[entry, plane, pl.ds(row, 1), :] = nothing

    @pl.when(xy == 0)
    def _():
        clear_row(-1, 0)

    @pl.when(xy == lax.axis_size("xy") - 1)
    def _():
        clear_row(1, 7)

    @pl.when(gz == 0)
    def _():
        out[0:9, 0] = jnp.zeros((9, 8, 128), jnp.float32)

    @pl.when(gz == lax.axis_size("gz") - 1)
    def _():
        out[18:27, 1] = jnp.zeros((9, 8, 128), jnp.float32)


def per_device(material, diffusivity, variation):
    vmem = pl.BlockSpec(memory_space=pltpu.VMEM)
    rho = pl.pallas_call(
        exchange_kernel,
        out_shape=jax.ShapeDtypeStruct((2, 7, 2, 2, 8, 128), jnp.float32),
        in_specs=[vmem, pl.BlockSpec(memory_space=pltpu.SMEM), vmem],
        out_specs=vmem,
        scratch_shapes=[
            pltpu.VMEM((4, 2, 16, 128), jnp.float32),
            pltpu.SemaphoreType.DMA((len(STEPS),)),
            pltpu.SemaphoreType.DMA((len(STEPS),)),
        ],
        compiler_params=pltpu.CompilerParams(collective_id=0, has_side_effects=True),
        name="exchange",
    )(material, diffusivity, variation)
    return pl.pallas_call(
        stencil_kernel,
        out_shape=jax.ShapeDtypeStruct((27, 2, 8, 128), jnp.float32),
        in_specs=[vmem],
        out_specs=vmem,
        name="stencil",
    )(rho)


def solution(mesh):
    placed = (P("gz", "xy", None), P(), P("gz", "xy", None))
    return jax.shard_map(
        per_device, mesh=mesh, in_specs=placed, out_specs=P(None, "gz", "xy", None), check_vma=False
    )
```

time: 332 us -> 22.1 us (0.07)
  the two profiles are of different devices: /device:TPU:34 before, /device:TPU:1 now
where the time goes in v1:
time: 22.1 us; the launch traced here: 21.9 us
  Pallas kernels  21.9 us (99%)
    pallas_call x1, Pallas kernels, per_device(): pl.pallas_call(exchange_kernel, out_shape=jax.ShapeDtypeStruct((2, 7, 2,...  19.9 us
    pallas_call x1, Pallas kernels, per_device(): pl.pallas_call(stencil_kernel, out_shape=jax.ShapeDtypeStruct((27, 2, 8,...  1.98 us

profile of v1, /device:TPU:1, one launch (start us, length us, event | category | flops | bytes accessed | tf_op | source)
XLA Modules:
  0.0 21.9 jit_solution(270977783862710174)
XLA Ops:
  0.0 19.9 %exchange.1.rho = f32[2,7,2,2,8,128]{5,4,3,2,1,0:T(8,128)} custom-call(s32[4,16,256]{2,1,0:T(8,128)} %material.1, f32[8]{0:T(128)} %diffusivity.1, f32[4,16,256]{2,1,0:T(8,128)} %variation.1), custom_call_target="tpu_custom_call" | custom-call | tf_op jit(solution)/shard_map/exchange/pallas_call | solution.py:444
  19.9 2.0 %stencil.1 = f32[27,2,8,128]{3,2,1,0:T(8,128)} custom-call(f32[2,7,2,2,8,128]{5,4,3,2,1,0:T(8,128)} %exchange.1.rho), custom_call_target="tpu_custom_call" | custom-call | tf_op jit(solution)/shard_map/stencil/pallas_call | solution.py:457

commit v2 on v1

--- a/solution.py
+++ b/solution.py
@@ -9,7 +9,7 @@
 
 MESH = pl.DeviceIdType.MESH
 OUTSIDE = -1e-18
-STEPS = [(dz, dx) for dz in (-1, 0, 1) for dx in (-1, 0, 1) if (dz, dx) != (0, 0)]
+ROW = 16
 
 
 class Rows:
@@ -320,7 +320,7 @@
 
 
 def split_lanes(value):
-    lane = lax.broadcasted_iota(jnp.int32, (16, 128), 1)
+    lane = lax.broadcasted_iota(jnp.int32, (value.shape[0], 128), 1)
     left, right = value[:, :128], value[:, 128:]
     first = (lane * 2) % 128 + lane // 64
     left = jnp.take_along_axis(left, first, axis=1)
@@ -330,61 +330,154 @@
     return even, odd
 
 
-def exchange_kernel(material, diffusivity, variation, out, split, send_sem, recv_sem):
+SENT = {-1: (0, 1), 0: (0, 4), 1: (2, 2)}
+LANDED = {-1: 6, 0: 2, 1: 0}
+AHEAD = [(0, 1), (-1, 1), (1, 1)]
+SIDE = [(-1, 0), (1, 0)]
+BACK = [(0, -1), (-1, -1), (1, -1)]
+MESSAGES = AHEAD + SIDE + BACK
+
+
+def exchange_kernel(
+    material, diffusivity, variation, out, blocks, facts, borders, edges, split, load_sem, send_sem, recv_sem
+):
     gz, xy = lax.axis_index("gz"), lax.axis_index("xy")
     count_z, count_x = lax.axis_size("gz"), lax.axis_size("xy")
+    inputs = (material, variation)
+    own = (blocks, facts)
+
+    def exists(dz, dx):
+        inside = None
+        for at, step, count in ((gz, dz, count_z), (xy, dx, count_x)):
+            if step:
+                good = at + step < count if step > 0 else at > 0
+                inside = good if inside is None else jnp.logical_and(inside, good)
+        return inside
 
     def device(dz, dx):
-        return {
-            "gz": lax.rem(gz + (dz + count_z), count_z),
-            "xy": lax.rem(xy + (dx + count_x), count_x),
-        }
+        return {"gz": gz + dz, "xy": xy + dx}
+
+    def copies(dz, dx):
+        n = MESSAGES.index((dz, dx))
+        first, planes = SENT[dz]
+        made = []
+        for which in (0, 1):
+            source = inputs[which].at[pl.ds(first, planes)]
+            if dx == 0:
+                target = borders[which].at[pl.ds(0 if dz > 0 else 2, planes)]
+            else:
+                row, rows, at = (14, 2, 6) if dx > 0 else (0, 1, 0)
+                source = inputs[which].at[pl.ds(first, planes), pl.ds(row, rows)]
+                target = edges[which].at[pl.ds(LANDED[dz], planes), pl.ds(at, rows)]
+            made.append(
+                pltpu.make_async_remote_copy(
+                    src_ref=source,
+                    dst_ref=target,
+                    send_sem=send_sem.at[n, which],
+                    recv_sem=recv_sem.at[n, which],
+                    device_id=device(dz, dx),
+                    device_id_type=MESH,
+                )
+            )
+        return made
+
+    def send(dz, dx, condition=None):
+        good = exists(dz, dx)
+
+        @pl.when(good if condition is None else jnp.logical_and(good, condition))
+        def _():
+            for copy in copies(dz, dx):
+                copy.start()
+
+    def receive(dz, dx):
+        @pl.when(exists(-dz, -dx))
+        def _():
+            for copy in copies(dz, dx):
+                copy.wait_recv()
 
     barrier = pltpu.get_barrier_semaphore()
-    for dz, dx in STEPS:
-        pl.semaphore_signal(barrier, inc=1, device_id=device(dz, dx), device_id_type=MESH)
+    last = jnp.logical_and(lax.rem(xy, ROW) == ROW - 1, xy < count_x - 1)
+
+    def greet(dz, dx, condition=None):
+        good = exists(dz, dx)
+
+        @pl.when(good if condition is None else jnp.logical_and(good, condition))
+        def _():
+            pl.semaphore_signal(barrier, inc=1, device_id=device(dz, dx), device_id_type=MESH)
+
+    for dz, dx in BACK:
+        greet(dz, dx)
+    for dz, dx in SIDE:
+        greet(dz, dx, jnp.logical_not(last))
+    loads = [pltpu.make_async_copy(inputs[n], own[n], load_sem.at[n]) for n in (0, 1)]
+    for copy in loads:
+        copy.start()
+    one = jnp.int32(1)
+    z_sides = jnp.where(gz > 0, one, 0) + jnp.where(gz < count_z - 1, one, 0)
+    expected = jnp.where(last, 0, z_sides) + jnp.where(xy < count_x - 1, z_sides + 1, 0)
+    pl.semaphore_wait(barrier, expected)
+    for dz, dx in AHEAD:
+        send(dz, dx)
+    for dz, dx in SIDE:
+        send(dz, dx, jnp.logical_not(last))
 
     table = [diffusivity[which] for which in range(8)]
-    for k in range(4):
-        which = material[k]
-        bits = [(which & bit) != 0 for bit in (1, 2, 4)]
+
+    def resistivity(which, factor):
         values = table
-        for bit in bits:
+        for bit in (1, 2, 4):
+            chosen = (which & bit) != 0
             values = [
-                jnp.where(bit, values[2 * n + 1], values[2 * n])
+                jnp.where(chosen, values[2 * n + 1], values[2 * n])
                 for n in range(len(values) // 2)
             ]
-        rho = -0.5 / (values[0] * variation[k])
-        for yp, half in enumerate(split_lanes(rho)):
-            split[k, yp] = half
+        return -0.5 / (values[0] * factor)
+
+    def place(plane, which, factor):
+        for yp, half in enumerate(split_lanes(resistivity(which, factor))):
+            split[plane, yp] = half
             for xp in (0, 1):
-                out[0, k + 2, xp, yp] = split[k, yp, pl.ds(xp, 8, stride=2), :]
-
-    pl.semaphore_wait(barrier, len(STEPS))
-    copies = []
-    for n, (dz, dx) in enumerate(STEPS):
-        source = {-1: pl.ds(2, 1), 0: pl.ds(2, 4), 1: pl.ds(4, 2)}[dz]
-        target = {-1: pl.ds(6, 1), 0: pl.ds(2, 4), 1: pl.ds(0, 2)}[dz]
-        if dx == 0:
-            src, dst = out.at[0, source], out.at[0, target]
-        elif dx == 1:
-            rows = (slice(None), slice(None), pl.ds(7, 1))
-            src, dst = out.at[(0, source) + rows], out.at[(1, target) + rows]
-        else:
-            rows = (0, slice(None), pl.ds(0, 1))
-            src, dst = out.at[(0, source) + rows], out.at[(1, target) + rows]
-        copy = pltpu.make_async_remote_copy(
-            src_ref=src,
-            dst_ref=dst,
-            send_sem=send_sem.at[n],
-            recv_sem=recv_sem.at[n],
-            device_id=device(dz, dx),
-            device_id_type=MESH,
-        )
-        copy.start()
-        copies.append(copy)
-    for copy in copies:
+                out[0, plane, xp, yp] = split[plane, yp, pl.ds(xp, 8, stride=2), :]
+
+    for copy in loads:
         copy.wait()
+    for k in range(4):
+        place(k + 2, blocks[k], facts[k])
+
+    @pl.when(last)
+    def _():
+        for dz, dx in AHEAD:
+            receive(dz, dx)
+        for dz, dx in BACK:
+            send(dz, dx)
+        for dz, dx in SIDE:
+            send(dz, dx)
+
+    for dz, dx in SIDE:
+        receive(dz, dx)
+    for n, plane in enumerate((0, 1, 6)):
+        place(plane, borders[0][n], borders[1][n])
+
+    @pl.when(jnp.logical_not(last))
+    def _():
+        for dz, dx in AHEAD:
+            receive(dz, dx)
+        for dz, dx in BACK:
+            send(dz, dx)
+
+    for dz, dx in BACK:
+        receive(dz, dx)
+    bottom = row_index() == 7
+    for plane in range(7):
+        halves = split_lanes(resistivity(edges[0][plane], edges[1][plane]))
+        for yp, half in enumerate(halves):
+            out[1, plane, 0, yp] = jnp.where(bottom, pltpu.roll(half, 1, 0), half)
+            out[1, plane, 1, yp] = half
+    for dz, dx in MESSAGES:
+        @pl.when(exists(dz, dx))
+        def _():
+            for copy in copies(dz, dx):
+                copy.wait_send()
 
     @pl.when(gz == 0)
     def _():
@@ -444,12 +537,21 @@
     rho = pl.pallas_call(
         exchange_kernel,
         out_shape=jax.ShapeDtypeStruct((2, 7, 2, 2, 8, 128), jnp.float32),
-        in_specs=[vmem, pl.BlockSpec(memory_space=pltpu.SMEM), vmem],
+        in_specs=[
+            pl.BlockSpec(memory_space=pltpu.HBM),
+            pl.BlockSpec(memory_space=pltpu.SMEM),
+            pl.BlockSpec(memory_space=pltpu.HBM),
+        ],
         out_specs=vmem,
         scratch_shapes=[
-            pltpu.VMEM((4, 2, 16, 128), jnp.float32),
-            pltpu.SemaphoreType.DMA((len(STEPS),)),
-            pltpu.SemaphoreType.DMA((len(STEPS),)),
+            pltpu.VMEM((4, 16, 256), jnp.int32),
+            pltpu.VMEM((4, 16, 256), jnp.float32),
+            [pltpu.VMEM((3, 16, 256), kind) for kind in (jnp.int32, jnp.float32)],
+            [pltpu.VMEM((7, 8, 256), kind) for kind in (jnp.int32, jnp.float32)],
+            pltpu.VMEM((7, 2, 16, 128), jnp.float32),
+            pltpu.SemaphoreType.DMA((2,)),
+            pltpu.SemaphoreType.DMA((len(MESSAGES), 2)),
+            pltpu.SemaphoreType.DMA((len(MESSAGES), 2)),
         ],
         compiler_params=pltpu.CompilerParams(collective_id=0, has_side_effects=True),
         name="exchange",

time: 22.1 us -> 18.1 us (0.82)
  the two profiles are of different devices: /device:TPU:1 before, /device:TPU:58 now
where the time goes in v2:
time: 18.1 us; the launch traced here: 17.9 us
  Pallas kernels  17.9 us (99%)
    pallas_call x1, Pallas kernels, per_device(): pl.pallas_call(exchange_kernel, out_shape=jax.ShapeDtypeStruct((2, 7, 2,...  16 us
    pallas_call x1, Pallas kernels, per_device(): pl.pallas_call(stencil_kernel, out_shape=jax.ShapeDtypeStruct((27, 2, 8,...  1.98 us

profile of v2, /device:TPU:58, one launch (start us, length us, event | category | flops | bytes accessed | tf_op | source)
XLA Modules:
  0.0 17.9 jit_solution(206200678046262857)
XLA Ops:
  0.0 16.0 %exchange.1.rho = f32[2,7,2,2,8,128]{5,4,3,2,1,0:T(8,128)} custom-call(s32[4,16,256]{2,1,0:T(8,128)} %material.1, f32[8]{0:T(128)} %diffusivity.1, f32[4,16,256]{2,1,0:T(8,128)} %variation.1), custom_call_target="tpu_custom_call" | custom-call | tf_op jit(solution)/shard_map/exchange/pallas_call | solution.py:537
  16.0 2.0 %stencil.1 = f32[27,2,8,128]{3,2,1,0:T(8,128)} custom-call(f32[2,7,2,2,8,128]{5,4,3,2,1,0:T(8,128)} %exchange.1.rho), custom_call_target="tpu_custom_call" | custom-call | tf_op jit(solution)/shard_map/stencil/pallas_call | solution.py:559

commit v3 on v2

--- a/solution.py
+++ b/solution.py
@@ -339,7 +339,7 @@
 
 
 def exchange_kernel(
-    material, diffusivity, variation, out, blocks, facts, borders, edges, split, load_sem, send_sem, recv_sem
+    material, diffusivity, variation, out, blocks, facts, borders, edges, split, load_sem, send_sem, recv_sem, here
 ):
     gz, xy = lax.axis_index("gz"), lax.axis_index("xy")
     count_z, count_x = lax.axis_size("gz"), lax.axis_size("xy")
@@ -396,30 +396,48 @@
                 copy.wait_recv()
 
     barrier = pltpu.get_barrier_semaphore()
-    last = jnp.logical_and(lax.rem(xy, ROW) == ROW - 1, xy < count_x - 1)
-
-    def greet(dz, dx, condition=None):
+    place_in_row = lax.rem(xy, ROW)
+    first = jnp.logical_and(place_in_row == 0, xy > 0)
+    last = jnp.logical_and(place_in_row == ROW - 1, xy < count_x - 1)
+    inner = jnp.logical_not(jnp.logical_or(first, last))
+    not_last = jnp.logical_not(last)
+    before_last = lax.rem(xy + 1, ROW) == ROW - 1
+    before_last = jnp.logical_and(before_last, xy < count_x - 2)
+
+    def greet(semaphore, dz, dx, condition=None):
         good = exists(dz, dx)
 
         @pl.when(good if condition is None else jnp.logical_and(good, condition))
         def _():
-            pl.semaphore_signal(barrier, inc=1, device_id=device(dz, dx), device_id_type=MESH)
+            pl.semaphore_signal(
+                semaphore, inc=1, device_id=device(dz, dx), device_id_type=MESH
+            )
 
     for dz, dx in BACK:
-        greet(dz, dx)
+        greet(barrier, dz, dx)
     for dz, dx in SIDE:
-        greet(dz, dx, jnp.logical_not(last))
+        greet(barrier, dz, dx, not_last)
+    for dz, dx in AHEAD:
+        greet(barrier, dz, dx, jnp.logical_not(jnp.logical_or(last, before_last)))
     loads = [pltpu.make_async_copy(inputs[n], own[n], load_sem.at[n]) for n in (0, 1)]
     for copy in loads:
         copy.start()
     one = jnp.int32(1)
     z_sides = jnp.where(gz > 0, one, 0) + jnp.where(gz < count_z - 1, one, 0)
-    expected = jnp.where(last, 0, z_sides) + jnp.where(xy < count_x - 1, z_sides + 1, 0)
+    expected = (
+        jnp.where(xy < count_x - 1, z_sides + 1, 0)
+        + jnp.where(last, 0, z_sides)
+        + jnp.where(jnp.logical_and(inner, xy > 0), z_sides + 1, 0)
+    )
     pl.semaphore_wait(barrier, expected)
+    for dz, dx in AHEAD:
+        greet(here, dz, dx, last)
     for dz, dx in AHEAD:
         send(dz, dx)
     for dz, dx in SIDE:
-        send(dz, dx, jnp.logical_not(last))
+        send(dz, dx, not_last)
+    for dz, dx in BACK:
+        send(dz, dx, inner)
 
     table = [diffusivity[which] for which in range(8)]
 
@@ -457,16 +475,20 @@
         receive(dz, dx)
     for n, plane in enumerate((0, 1, 6)):
         place(plane, borders[0][n], borders[1][n])
-
-    @pl.when(jnp.logical_not(last))
+    for dz, dx in BACK:
+        receive(dz, dx)
+
+    @pl.when(first)
+    def _():
+        pl.semaphore_wait(here, z_sides + 1)
+        for dz, dx in BACK:
+            send(dz, dx)
+
+    @pl.when(not_last)
     def _():
         for dz, dx in AHEAD:
             receive(dz, dx)
-        for dz, dx in BACK:
-            send(dz, dx)
-
-    for dz, dx in BACK:
-        receive(dz, dx)
+
     bottom = row_index() == 7
     for plane in range(7):
         halves = split_lanes(resistivity(edges[0][plane], edges[1][plane]))
@@ -552,6 +574,7 @@
             pltpu.SemaphoreType.DMA((2,)),
             pltpu.SemaphoreType.DMA((len(MESSAGES), 2)),
             pltpu.SemaphoreType.DMA((len(MESSAGES), 2)),
+            pltpu.SemaphoreType.REGULAR,
         ],
         compiler_params=pltpu.CompilerParams(collective_id=0, has_side_effects=True),
         name="exchange",

time: 18.1 us -> 16.8 us (0.928)
  Pallas kernels: 17.9 us -> 16.6 us
    pallas_call x1, Pallas kernels: 16 us -> 14.6 us  [per_device(): pl.pallas_call(exchange_kernel, out_shape=jax.ShapeDtypeStruct((2, 7, 2,...]
where the time goes in v3:
time: 16.8 us; the launch traced here: 16.6 us
  Pallas kernels  16.6 us (99%)
    pallas_call x1, Pallas kernels, per_device(): pl.pallas_call(exchange_kernel, out_shape=jax.ShapeDtypeStruct((2, 7, 2,...  14.6 us
    pallas_call x1, Pallas kernels, per_device(): pl.pallas_call(stencil_kernel, out_shape=jax.ShapeDtypeStruct((27, 2, 8,...  1.98 us

profile of v3, /device:TPU:58, one launch (start us, length us, event | category | flops | bytes accessed | tf_op | source)
XLA Modules:
  0.0 16.6 jit_solution(1303085877169650962)
XLA Ops:
  0.0 14.6 %exchange.1.rho = f32[2,7,2,2,8,128]{5,4,3,2,1,0:T(8,128)} custom-call(s32[4,16,256]{2,1,0:T(8,128)} %material.1, f32[8]{0:T(128)} %diffusivity.1, f32[4,16,256]{2,1,0:T(8,128)} %variation.1), custom_call_target="tpu_custom_call" | custom-call | tf_op jit(solution)/shard_map/exchange/pallas_call | solution.py:559
  14.6 2.0 %stencil.1 = f32[27,2,8,128]{3,2,1,0:T(8,128)} custom-call(f32[2,7,2,2,8,128]{5,4,3,2,1,0:T(8,128)} %exchange.1.rho), custom_call_target="tpu_custom_call" | custom-call | tf_op jit(solution)/shard_map/stencil/pallas_call | solution.py:582

commit v4 on v3

--- a/solution.py
+++ b/solution.py
@@ -10,6 +10,7 @@
 MESH = pl.DeviceIdType.MESH
 OUTSIDE = -1e-18
 ROW = 16
+VMEM_BYTES = 4 << 20
 
 
 class Rows:
@@ -332,19 +333,18 @@
 
 SENT = {-1: (0, 1), 0: (0, 4), 1: (2, 2)}
 LANDED = {-1: 6, 0: 2, 1: 0}
-AHEAD = [(0, 1), (-1, 1), (1, 1)]
+AHEAD = [(-1, 1), (1, 1), (0, 1)]
 SIDE = [(-1, 0), (1, 0)]
 BACK = [(0, -1), (-1, -1), (1, -1)]
 MESSAGES = AHEAD + SIDE + BACK
 
 
 def exchange_kernel(
-    material, diffusivity, variation, out, blocks, facts, borders, edges, split, load_sem, send_sem, recv_sem, here
+    material, diffusivity, variation, out, blocks, facts, levels, borders, edges, split, load_sem, send_sem, recv_sem, here
 ):
     gz, xy = lax.axis_index("gz"), lax.axis_index("xy")
     count_z, count_x = lax.axis_size("gz"), lax.axis_size("xy")
     inputs = (material, variation)
-    own = (blocks, facts)
 
     def exists(dz, dx):
         inside = None
@@ -419,7 +419,12 @@
         greet(barrier, dz, dx, not_last)
     for dz, dx in AHEAD:
         greet(barrier, dz, dx, jnp.logical_not(jnp.logical_or(last, before_last)))
-    loads = [pltpu.make_async_copy(inputs[n], own[n], load_sem.at[n]) for n in (0, 1)]
+    loads = [
+        pltpu.make_async_copy(source, target, load_sem.at[n])
+        for n, (source, target) in enumerate(
+            ((material, blocks), (variation, facts), (diffusivity, levels))
+        )
+    ]
     for copy in loads:
         copy.start()
     one = jnp.int32(1)
@@ -439,8 +444,6 @@
     for dz, dx in BACK:
         send(dz, dx, inner)
 
-    table = [diffusivity[which] for which in range(8)]
-
     def resistivity(which, factor):
         values = table
         for bit in (1, 2, 4):
@@ -459,6 +462,7 @@
 
     for copy in loads:
         copy.wait()
+    table = [levels[which] for which in range(8)]
     for k in range(4):
         place(k + 2, blocks[k], facts[k])
 
@@ -556,27 +560,34 @@
 
 def per_device(material, diffusivity, variation):
     vmem = pl.BlockSpec(memory_space=pltpu.VMEM)
+    material, diffusivity, variation = (
+        pltpu.with_memory_space_constraint(x, pltpu.HBM)
+        for x in (material, diffusivity, variation)
+    )
     rho = pl.pallas_call(
         exchange_kernel,
         out_shape=jax.ShapeDtypeStruct((2, 7, 2, 2, 8, 128), jnp.float32),
         in_specs=[
             pl.BlockSpec(memory_space=pltpu.HBM),
-            pl.BlockSpec(memory_space=pltpu.SMEM),
+            pl.BlockSpec(memory_space=pltpu.HBM),
             pl.BlockSpec(memory_space=pltpu.HBM),
         ],
         out_specs=vmem,
         scratch_shapes=[
             pltpu.VMEM((4, 16, 256), jnp.int32),
             pltpu.VMEM((4, 16, 256), jnp.float32),
+            pltpu.SMEM((8,), jnp.float32),
             [pltpu.VMEM((3, 16, 256), kind) for kind in (jnp.int32, jnp.float32)],
             [pltpu.VMEM((7, 8, 256), kind) for kind in (jnp.int32, jnp.float32)],
             pltpu.VMEM((7, 2, 16, 128), jnp.float32),
-            pltpu.SemaphoreType.DMA((2,)),
+            pltpu.SemaphoreType.DMA((3,)),
             pltpu.SemaphoreType.DMA((len(MESSAGES), 2)),
             pltpu.SemaphoreType.DMA((len(MESSAGES), 2)),
             pltpu.SemaphoreType.REGULAR,
         ],
-        compiler_params=pltpu.CompilerParams(collective_id=0, has_side_effects=True),
+        compiler_params=pltpu.CompilerParams(
+            collective_id=0, has_side_effects=True, vmem_limit_bytes=VMEM_BYTES
+        ),
         name="exchange",
     )(material, diffusivity, variation)
     return pl.pallas_call(
@@ -584,6 +595,7 @@
         out_shape=jax.ShapeDtypeStruct((27, 2, 8, 128), jnp.float32),
         in_specs=[vmem],
         out_specs=vmem,
+        compiler_params=pltpu.CompilerParams(vmem_limit_bytes=VMEM_BYTES),
         name="stencil",
     )(rho)
 

time: 16.8 us -> 14.3 us (0.85)
  Pallas kernels: 16.6 us -> 14.1 us
    pallas_call x1, Pallas kernels: 14.6 us -> 13.1 us  [per_device(): pl.pallas_call(exchange_kernel, out_shape=jax.ShapeDtypeStruct((2, 7, 2,...]
    pallas_call x1, Pallas kernels: 1.98 us -> 1.04 us  [per_device(): pl.pallas_call(stencil_kernel, out_shape=jax.ShapeDtypeStruct((27, 2, 8,...]
where the time goes in v4:
time: 14.3 us; the launch traced here: 14.1 us
  Pallas kernels  14.1 us (99%)
    pallas_call x1, Pallas kernels, per_device(): pl.pallas_call(exchange_kernel, out_shape=jax.ShapeDtypeStruct((2, 7, 2,...  13.1 us
    pallas_call x1, Pallas kernels, per_device(): pl.pallas_call(stencil_kernel, out_shape=jax.ShapeDtypeStruct((27, 2, 8,...  1.04 us

profile of v4, /device:TPU:58, one launch (start us, length us, event | category | flops | bytes accessed | tf_op | source)
XLA Modules:
  0.0 14.1 jit_solution(13896792707285520593)
XLA Ops:
  0.0 13.1 %exchange.1.rho = f32[2,7,2,2,8,128]{5,4,3,2,1,0:T(8,128)S(1)} custom-call(s32[4,16,256]{2,1,0:T(8,128)} %material.1, f32[8]{0:T(128)} %diffusivity.1, f32[4,16,256]{2,1,0:T(8,128)} %variation.1), custom_call_target="tpu_custom_call" | custom-call | tf_op jit(solution)/shard_map/exchange/pallas_call | solution.py:567
  13.1 1.0 %stencil.1 = f32[27,2,8,128]{3,2,1,0:T(8,128)} custom-call(f32[2,7,2,2,8,128]{5,4,3,2,1,0:T(8,128)S(1)} %exchange.1.rho), custom_call_target="tpu_custom_call" | custom-call | tf_op jit(solution)/shard_map/stencil/pallas_call | solution.py:593

commit v5 on v4

v5 whole, which is shorter than its diff:
```python
import functools

import jax
import jax.numpy as jnp
from jax import lax
from jax.experimental import pallas as pl
from jax.experimental.pallas import tpu as pltpu
from jax.sharding import PartitionSpec as P

MESH = pl.DeviceIdType.MESH
OUTSIDE = -1e-18
ROW = 16
VMEM_BYTES = 4 << 20


def row_index():
    return lax.broadcasted_iota(jnp.int32, (8, 128), 0)


def lane_index():
    return lax.broadcasted_iota(jnp.int32, (8, 128), 1)


def previous_row(value):
    return jnp.where(row_index() == 0, 0.0, pltpu.roll(value, 1, 0))


def next_lane(value):
    return pltpu.roll(value, 127, 1)


def previous_lane(value):
    return pltpu.roll(value, 1, 1)


def next_lane_bounded(value):
    return jnp.where(lane_index() == 127, OUTSIDE, next_lane(value))


def without_last(value):
    return jnp.where(lane_index() == 127, 0.0, value)


def inverse(value):
    return 1.0 / value


class Group:
    def __init__(self, **arrays):
        self.__dict__.update(arrays)

    def moved(self, step):
        def roll(value):
            if isinstance(value, (tuple, list)):
                return tuple(roll(part) for part in value)
            return value if value is None else pltpu.roll(value, -step % 8, 0)

        return Group(**{name: roll(value) for name, value in self.__dict__.items()})


def x_weights(even, odd, even_next):
    low, high, link = [], [], []
    for yp in (0, 1):
        before = even[yp] + odd[yp]
        after = odd[yp] + even_next[yp]
        scale = inverse(before + after)
        low.append(after * scale)
        high.append(before * scale)
        link.append(scale)
    return {"low": low, "high": high, "link": link, "odd": odd, "even": even}


def y_weights(even):
    before = even[0] + even[1]
    after = even[1] + next_lane_bounded(even[0])
    scale = inverse(before + after)
    return after * scale, without_last(before * scale), before, after


def z_link(lower, upper, edge):
    steps = []
    faces = []
    for yp in (0, 1):
        odd = inverse(lower.odd[yp] + upper.odd[yp])
        low, high = lower.low[yp] * odd, lower.high[yp] * odd
        same = high * upper.high[yp]
        even = None
        if not edge:
            even = inverse(lower.even[yp] + upper.even[yp])
            same = even + low * upper.low[yp] + previous_row(same)
        steps.append((same, low * upper.high[yp], high * upper.low[yp]))
        faces.append((even, odd))
    (even_same, even_up, even_down), (odd_same, odd_up, odd_down) = steps

    def y_step(even, odd, lower_y, upper_y):
        first, second = lower_y[0] * odd, lower_y[1] * odd
        return (
            even + first * upper_y[0] + previous_lane(second * upper_y[1]),
            first * upper_y[1],
            second * upper_y[0],
        )

    return Group(
        faces=tuple(faces),
        same=y_step(even_same, odd_same, lower.y_same, upper.y_same),
        up=y_step(even_up, odd_up, lower.y, upper.y_next),
        down=y_step(even_down, odd_down, lower.y_next, upper.y),
    )


def within(plane, faces_below, faces_above, edge):
    odd_e, odd_o = plane.odd

    def lower_face(face, rho):
        return jnp.where(lane_index() == 0, inverse(rho + OUTSIDE), previous_lane(face))

    odd_before = inverse(odd_e + odd_o)
    odd_after = inverse(odd_o + next_lane_bounded(odd_e))
    odd_sum = [
        odd_before + lower_face(odd_after, odd_e) + faces_below[0][1] + faces_above[0][1],
        odd_before + odd_after + faces_below[1][1] + faces_above[1][1],
    ]
    odd_after = without_last(odd_after)
    if not edge:
        even_before, even_after = inverse(plane.before), inverse(plane.after)
        even_lower = lower_face(even_after, plane.even[0])
        even_sum = [
            even_before + even_lower + faces_below[0][0] + faces_above[0][0],
            even_before + even_after + faces_below[1][0] + faces_above[1][0],
        ]
        even_after = without_last(even_after)
    centre, along = [], []
    for yp in (0, 1):
        low, high, link = plane.low[yp], plane.high[yp], plane.link[yp]
        low_sum, high_sum = low * odd_sum[yp], high * odd_sum[yp]
        value = link + high_sum * high
        if not edge:
            value = even_sum[yp] + (link + low_sum * low) + previous_row(value)
        centre.append(value)
        along.append(link - low_sum * high)
    low_e, low_o = plane.low
    high_e, high_o = plane.high
    low_n, high_n = next_lane(low_e), next_lane(high_e)
    first, second = low_o * odd_before, high_o * odd_before
    before = (second * high_e, second * low_e, first * high_e)
    if not edge:
        before = (even_before + first * low_e + previous_row(before[0]),) + before[1:]
    first, second = low_o * odd_after, high_o * odd_after
    after = (second * high_n, first * high_n, second * low_n)
    if not edge:
        after = (even_after + first * low_n + previous_row(after[0]),) + after[1:]
    low, high = plane.y_same
    cross = low * centre[1]
    side = high * before[0] + low * after[0] - cross * high
    middle = (
        centre[0]
        + low * (cross - before[0] - before[0])
        + previous_lane(high * (high * centre[1] - after[0] - after[0]))
    )
    low, high = plane.y
    low_next, high_next = plane.y_next
    one = low * along[1] + before[1]
    two = high * along[1] + after[2]
    up = (
        along[0]
        + low_next * one
        + low * before[2]
        + previous_lane(high_next * two + high * after[1]),
        high_next * one + low * after[1],
        low_next * two + high * before[2],
    )
    return Group(centre=middle, side=side, up=up)


def z_weights(below, middle, above):
    before = below + middle
    after = middle + above
    scale = inverse(before + after)
    return after * scale, before * scale


def with_lanes(value, value_next):
    return (value, next_lane(value), value_next, next_lane(value_next))


def between(weights, inner, low_link, high_link):
    lo, lo_j, lo_i, lo_ij = weights.lo
    hi, hi_j, hi_i, hi_ij = weights.hi
    (lo_s, lo_sj), (hi_s, hi_sj) = weights.lo_same, weights.hi_same

    def term(first, second, low, high, own):
        return second * (low + first * own) + first * high

    same = (
        hi_s * (low_link.same[0] - lo_s * inner.centre) + lo_s * high_link.same[0],
        term(lo_s, hi_sj, low_link.same[1], high_link.same[1], inner.side),
        term(lo_sj, hi_s, low_link.same[2], high_link.same[2], inner.side),
    )
    up = (
        term(lo, hi_i, low_link.up[0], high_link.up[0], inner.up[0]),
        term(lo, hi_ij, low_link.up[1], high_link.up[1], inner.up[1]),
        term(lo_j, hi_i, low_link.up[2], high_link.up[2], inner.up[2]),
    )
    down = (
        term(lo_i, hi, low_link.down[0], high_link.down[0], inner.up[0]),
        term(lo_i, hi_j, low_link.down[1], high_link.down[1], inner.up[2]),
        term(lo_ij, hi, low_link.down[2], high_link.down[2], inner.up[1]),
    )
    return same, up, down


def level(own, below, above):
    centre, side = own.centre, own.side
    up = list(own.up)
    weights, inner, link = below
    hi, hi_j, hi_i, hi_ij = weights.hi
    hi_s, hi_sj = weights.hi_same
    centre = centre + hi_s * (hi_s * inner.centre - link.same[0] - link.same[0])
    side = side + hi_s * (hi_sj * inner.side + link.same[1]) + hi_sj * link.same[2]
    up[0] = up[0] + hi * (hi_i * inner.up[0] + link.up[0]) + hi_i * link.down[0]
    up[1] = up[1] + hi * (hi_ij * inner.up[1] + link.up[1]) + hi_ij * link.down[2]
    up[2] = up[2] + hi_j * (hi_i * inner.up[2] + link.up[2]) + hi_i * link.down[1]
    weights, inner, link = above
    lo, lo_j, lo_i, lo_ij = weights.lo
    lo_s, lo_sj = weights.lo_same
    centre = centre + lo_s * (lo_s * inner.centre - link.same[0] - link.same[0])
    side = side + lo_sj * (lo_s * inner.side + link.same[1]) + lo_s * link.same[2]
    up[0] = up[0] + lo_i * (lo * inner.up[0] + link.up[0]) + lo * link.down[0]
    up[1] = up[1] + lo_ij * (lo * inner.up[1] + link.up[1]) + lo * link.down[2]
    up[2] = up[2] + lo_i * (lo_j * inner.up[2] + link.up[2]) + lo_j * link.down[1]
    return centre, side, up


def own_part(load, beyond, store):
    last = row_index() == 7

    def next_row(value, packed, p):
        return jnp.where(last, packed[p : p + 1, :], pltpu.roll(value, 7, 0))

    y_beyond = y_weights(beyond)[:2]
    z_beyond = z_weights(pltpu.roll(beyond[0], 1, 0), beyond[0], pltpu.roll(beyond[0], 7, 0))
    planes = []
    for p in range(7):
        even, odd = ([load(p, xp, yp) for yp in (0, 1)] for xp in (0, 1))
        even_next = [next_row(even[yp], beyond[yp], p) for yp in (0, 1)]
        low, high, before, after = y_weights(even)
        planes.append(
            Group(
                before=before,
                after=after,
                y=(low, high),
                y_same=(low, high),
                y_next=(next_row(low, y_beyond[0], p), next_row(high, y_beyond[1], p)),
                **x_weights(even, odd, even_next),
            )
        )
    links = [z_link(planes[p], planes[p + 1], False) for p in range(6)]
    inner = [None] * 7
    for p in range(1, 6):
        inner[p] = within(planes[p], links[p - 1].faces, links[p].faces, False)
    weights = [None] * 7
    for p in (1, 3, 5):
        lo, hi = z_weights(*(planes[p + n].even[0] for n in (-1, 0, 1)))
        lo = with_lanes(lo, next_row(lo, z_beyond[0], p))
        hi = with_lanes(hi, next_row(hi, z_beyond[1], p))
        weights[p] = Group(lo=lo, hi=hi, lo_same=lo[:2], hi_same=hi[:2])
    for p in (1, 3, 5):
        same, up, down = between(weights[p], inner[p], links[p - 1], links[p])
        plane = (p - 1) // 2
        if plane < 2:
            low = functools.partial(store, -1)
            low(0, 0, plane, same[0])
            low(0, 1, plane, same[2])
            low(0, -1, plane, previous_lane(same[1]))
            low(1, 0, plane, down[0])
            low(1, 1, plane, down[2])
            low(1, -1, plane, previous_lane(down[1]))
            low(-1, 0, plane, previous_row(up[0]))
            low(-1, 1, plane, previous_row(up[2]))
            low(-1, -1, plane, previous_lane(previous_row(up[1])))
        if plane > 0:
            high = functools.partial(store, 1)
            high(0, 0, plane - 1, same[0])
            high(0, 1, plane - 1, same[1])
            high(0, -1, plane - 1, previous_lane(same[2]))
            high(1, 0, plane - 1, up[0])
            high(1, 1, plane - 1, up[1])
            high(1, -1, plane - 1, previous_lane(up[2]))
            high(-1, 0, plane - 1, previous_row(down[0]))
            high(-1, 1, plane - 1, previous_row(down[1]))
            high(-1, -1, plane - 1, previous_lane(previous_row(down[2])))
    for plane in (0, 1):
        p = 2 * plane + 2
        centre, side, up = level(
            inner[p],
            (weights[p - 1], inner[p - 1], links[p - 1]),
            (weights[p + 1], inner[p + 1], links[p]),
        )
        here = functools.partial(store, 0)
        here(0, 0, plane, -centre)
        here(0, 1, plane, side)
        here(0, -1, plane, previous_lane(side))
        here(1, 0, plane, up[0])
        here(-1, 0, plane, previous_row(up[0]))
        here(1, 1, plane, up[1])
        here(-1, -1, plane, previous_lane(previous_row(up[1])))
        here(1, -1, plane, previous_lane(up[2]))
        here(-1, 1, plane, previous_row(up[2]))


def edge_part(even, odd, even_next, merge):
    low_next, high_next = y_weights(even_next)[:2]
    y_next = (low_next, high_next)
    plane = Group(
        y=y_weights(even)[:2],
        y_same=y_next,
        y_next=y_next,
        **x_weights(even, odd, even_next),
    )
    link = z_link(plane, plane.moved(1), True)
    link_below = link.moved(-1)
    inner = within(plane, link_below.faces, link.faces, True)

    def around(value):
        return (pltpu.roll(value, 1, 0), value, pltpu.roll(value, 7, 0))

    own, following = z_weights(*around(even[0])), z_weights(*around(even_next[0]))
    lo, hi = (with_lanes(own[n], following[n]) for n in (0, 1))
    weights = Group(lo=lo, hi=hi, lo_same=lo[2:], hi_same=hi[2:])
    same, up, down = between(weights, inner, link_below, link)
    centre, side, inside = level(
        inner,
        (weights.moved(-1), inner.moved(-1), link_below),
        (weights.moved(1), inner.moved(1), link),
    )
    rows = (1, 3)
    merge(-1, 0, 0, same[0], rows)
    merge(-1, 0, 1, same[2], rows)
    merge(-1, 0, -1, previous_lane(same[1]), rows)
    merge(-1, -1, 0, up[0], rows)
    merge(-1, -1, 1, up[2], rows)
    merge(-1, -1, -1, previous_lane(up[1]), rows)
    rows = (3, 5)
    merge(1, 0, 0, same[0], rows)
    merge(1, 0, 1, same[1], rows)
    merge(1, 0, -1, previous_lane(same[2]), rows)
    merge(1, -1, 0, down[0], rows)
    merge(1, -1, 1, down[1], rows)
    merge(1, -1, -1, previous_lane(down[2]), rows)
    rows = (2, 4)
    merge(0, 0, 0, -centre, rows)
    merge(0, 0, 1, side, rows)
    merge(0, 0, -1, previous_lane(side), rows)
    merge(0, -1, 0, inside[0], rows)
    merge(0, -1, -1, previous_lane(inside[1]), rows)
    merge(0, -1, 1, inside[2], rows)


def split_lanes(value):
    lane = lax.broadcasted_iota(jnp.int32, (value.shape[0], 128), 1)
    left, right = value[:, :128], value[:, 128:]
    first = (lane * 2) % 128 + lane // 64
    left = jnp.take_along_axis(left, first, axis=1)
    right = jnp.take_along_axis(right, (first + 1) % 2 + first // 2 * 2, axis=1)
    even = jnp.where(lane < 64, left, right)
    odd = pltpu.roll(jnp.where(lane < 64, right, left), 64, 1)
    return even, odd


SENT = {-1: (0, 1), 0: (0, 4), 1: (2, 2)}
LANDED = {-1: 6, 0: 2, 1: 0}
AHEAD = [(-1, 1), (1, 1), (0, 1)]
SIDE = [(-1, 0), (1, 0)]
BACK = [(0, -1), (-1, -1), (1, -1)]
MESSAGES = AHEAD + SIDE + BACK


def exchange_kernel(
    material,
    diffusivity,
    variation,
    out,
    blocks,
    facts,
    levels,
    borders,
    edges,
    split,
    tiles,
    beyond,
    load_sem,
    send_sem,
    recv_sem,
    here,
):
    gz, xy = lax.axis_index("gz"), lax.axis_index("xy")
    count_z, count_x = lax.axis_size("gz"), lax.axis_size("xy")
    inputs = (material, variation)

    def exists(dz, dx):
        inside = None
        for at, step, count in ((gz, dz, count_z), (xy, dx, count_x)):
            if step:
                good = at + step < count if step > 0 else at > 0
                inside = good if inside is None else jnp.logical_and(inside, good)
        return inside

    def device(dz, dx):
        return {"gz": gz + dz, "xy": xy + dx}

    def copies(dz, dx, origin=None):
        origin = inputs if origin is None else origin
        n = MESSAGES.index((dz, dx))
        first, planes = SENT[dz]
        made = []
        for which in (0, 1):
            source = origin[which].at[pl.ds(first, planes)]
            if dx == 0:
                target = borders[which].at[pl.ds(0 if dz > 0 else 2, planes)]
            else:
                row, rows, at = (14, 2, 6) if dx > 0 else (0, 1, 0)
                source = origin[which].at[pl.ds(first, planes), pl.ds(row, rows)]
                target = edges[0 if dx > 0 else 1][which].at[pl.ds(LANDED[dz], planes), pl.ds(at, rows)]
            made.append(
                pltpu.make_async_remote_copy(
                    src_ref=source,
                    dst_ref=target,
                    send_sem=send_sem.at[n, which],
                    recv_sem=recv_sem.at[n, which],
                    device_id=device(dz, dx),
                    device_id_type=MESH,
                )
            )
        return made

    def send(dz, dx, origin=None):
        @pl.when(exists(dz, dx))
        def _():
            for copy in copies(dz, dx, origin):
                copy.start()

    def receive(dz, dx):
        @pl.when(exists(-dz, -dx))
        def _():
            for copy in copies(dz, dx):
                copy.wait_recv()

    barrier = pltpu.get_barrier_semaphore()
    place_in_row = lax.rem(xy, ROW)
    first = jnp.logical_and(place_in_row == 0, xy > 0)
    last = jnp.logical_and(place_in_row == ROW - 1, xy < count_x - 1)
    inner = jnp.logical_not(jnp.logical_or(first, last))
    not_last = jnp.logical_not(last)
    before_last = lax.rem(xy + 1, ROW) == ROW - 1
    before_last = jnp.logical_and(before_last, xy < count_x - 2)

    def greet(semaphore, dz, dx, condition=None):
        good = exists(dz, dx)

        @pl.when(good if condition is None else jnp.logical_and(good, condition))
        def _():
            pl.semaphore_signal(
                semaphore, inc=1, device_id=device(dz, dx), device_id_type=MESH
            )

    loads = [
        pltpu.make_async_copy(source, target, load_sem.at[n])
        for n, (source, target) in enumerate(
            ((material, blocks), (variation, facts), (diffusivity, levels))
        )
    ]
    one = jnp.int32(1)
    z_sides = jnp.where(gz > 0, one, 0) + jnp.where(gz < count_z - 1, one, 0)

    @pl.when(last)
    def _():
        pl.semaphore_wait(barrier, z_sides + 1)
        for dz, dx in AHEAD:
            greet(here, dz, dx)
        for dz, dx in AHEAD:
            send(dz, dx)
        for dz, dx in BACK:
            greet(barrier, dz, dx)
        for copy in loads:
            copy.start()

    @pl.when(not_last)
    def _():
        for dz, dx in BACK + SIDE:
            greet(barrier, dz, dx)
        for dz, dx in AHEAD:
            greet(barrier, dz, dx, jnp.logical_not(before_last))
        for copy in loads:
            copy.start()
        expected = (
            z_sides
            + jnp.where(xy < count_x - 1, z_sides + 1, 0)
            + jnp.where(jnp.logical_and(inner, xy > 0), z_sides + 1, 0)
        )
        pl.semaphore_wait(barrier, expected)
        for dz, dx in AHEAD + SIDE:
            send(dz, dx)

    @pl.when(inner)
    def _():
        for dz, dx in BACK:
            send(dz, dx)

    def resistivity(which, factor):
        values = table
        for bit in (1, 2, 4):
            chosen = (which & bit) != 0
            values = [
                jnp.where(chosen, values[2 * n + 1], values[2 * n])
                for n in range(len(values) // 2)
            ]
        return -0.5 / (values[0] * factor)

    def place(plane, which, factor):
        for yp, half in enumerate(split_lanes(resistivity(which, factor))):
            split[plane, yp] = half
            for xp in (0, 1):
                rows = split[plane, yp, pl.ds(xp, 8, stride=2), :]
                tiles[xp, yp, pl.ds(8 * plane, 8), :] = rows

    for copy in loads:
        copy.wait()
    table = [levels[which] for which in range(8)]
    for k in range(4):
        place(k + 2, blocks[k], facts[k])

    @pl.when(last)
    def _():
        for dz, dx in AHEAD:
            receive(dz, dx)
        for dz, dx in BACK:
            send(dz, dx)
        for dz, dx in SIDE:
            send(dz, dx)

    for dz, dx in SIDE:
        receive(dz, dx)
    for n, plane in enumerate((0, 1, 6)):
        place(plane, borders[0][n], borders[1][n])
    for dz, dx in BACK:
        receive(dz, dx)

    @pl.when(gz == 0)
    def _():
        tiles[:, :, pl.ds(0, 16), :] = jnp.full((2, 2, 16, 128), OUTSIDE, jnp.float32)

    @pl.when(gz == count_z - 1)
    def _():
        tiles[:, :, pl.ds(48, 8), :] = jnp.full((2, 2, 8, 128), OUTSIDE, jnp.float32)

    outside = jnp.logical_or(
        jnp.logical_and(gz == 0, row_index() < 2),
        jnp.logical_and(gz == count_z - 1, row_index() == 6),
    )

    def spread(side):
        for plane in range(7):
            which, factor = (kind[plane] for kind in edges[side])
            for yp, half in enumerate(split_lanes(resistivity(which, factor))):
                beyond[side, yp, pl.ds(8 * plane, 8), :] = half

    def packed(side, row, missing):
        missing = jnp.logical_or(outside, missing)
        return [
            jnp.where(missing, OUTSIDE, beyond[side, yp, pl.ds(row, 8, stride=8), :])
            for yp in (0, 1)
        ]

    def entry(dz, dx, dy):
        return 9 * (dz + 1) + 3 * (dx + 1) + dy + 1

    def load(p, xp, yp):
        return tiles[xp, yp, pl.ds(8 * p, 8), :]

    def store(dz, dx, dy, plane, value):
        out[entry(dz, dx, dy), plane] = value

    spread(1)
    own_part(load, packed(1, 0, xy == count_x - 1), store)

    @pl.when(xy == count_x - 1)
    def _():
        for dz in (-1, 0, 1):
            for dy in (-1, 0, 1):
                for plane in (0, 1):
                    nothing = jnp.zeros((1, 128), jnp.float32)
                    out[entry(dz, 1, dy), plane, pl.ds(7, 1), :] = nothing

    @pl.when(first)
    def _():
        pl.semaphore_wait(here, z_sides + 1)
        for dz, dx in BACK:
            send(dz, dx, (blocks, facts))

    @pl.when(not_last)
    def _():
        for dz, dx in AHEAD:
            receive(dz, dx)

    spread(0)
    even_next = [tiles[0, yp, pl.ds(0, 8, stride=8), :] for yp in (0, 1)]

    def merge(dz, dx, dy, value, rows):
        if dx:
            value = jnp.where(xy > 0, value, 0.0)
        for plane, row in enumerate(rows):
            at = (entry(dz, dx, dy), plane, pl.ds(0, 1), slice(None))
            piece = value[row : row + 1, :]
            out[at] = piece if dx else out[at] + piece

    edge_part(packed(0, 6, xy == 0), packed(0, 7, xy == 0), even_next, merge)

    @pl.when(gz == 0)
    def _():
        out[0:9, 0] = jnp.zeros((9, 8, 128), jnp.float32)

    @pl.when(gz == count_z - 1)
    def _():
        out[18:27, 1] = jnp.zeros((9, 8, 128), jnp.float32)

    for dz, dx in MESSAGES:
        @pl.when(exists(dz, dx))
        def _():
            for copy in copies(dz, dx):
                copy.wait_send()


def write_kernel(result, out, sem):
    copy = pltpu.make_async_copy(result, out, sem.at[0])
    copy.start()
    copy.wait()


def per_device(material, diffusivity, variation):
    vmem = pl.BlockSpec(memory_space=pltpu.VMEM)
    material, diffusivity, variation = (
        pltpu.with_memory_space_constraint(x, pltpu.HBM)
        for x in (material, diffusivity, variation)
    )
    result = pl.pallas_call(
        exchange_kernel,
        out_shape=jax.ShapeDtypeStruct((27, 2, 8, 128), jnp.float32),
        in_specs=[
            pl.BlockSpec(memory_space=pltpu.HBM),
            pl.BlockSpec(memory_space=pltpu.HBM),
            pl.BlockSpec(memory_space=pltpu.HBM),
        ],
        out_specs=vmem,
        scratch_shapes=[
            pltpu.VMEM((4, 16, 256), jnp.int32),
            pltpu.VMEM((4, 16, 256), jnp.float32),
            pltpu.SMEM((8,), jnp.float32),
            [pltpu.VMEM((3, 16, 256), kind) for kind in (jnp.int32, jnp.float32)],
            [
                [pltpu.VMEM((7, 8, 256), kind) for kind in (jnp.int32, jnp.float32)]
                for _ in range(2)
            ],
            pltpu.VMEM((7, 2, 16, 128), jnp.float32),
            pltpu.VMEM((2, 2, 64, 128), jnp.float32),
            pltpu.VMEM((2, 2, 64, 128), jnp.float32),
            pltpu.SemaphoreType.DMA((3,)),
            pltpu.SemaphoreType.DMA((len(MESSAGES), 2)),
            pltpu.SemaphoreType.DMA((len(MESSAGES), 2)),
            pltpu.SemaphoreType.REGULAR,
        ],
        compiler_params=pltpu.CompilerParams(
            collective_id=0, has_side_effects=True, vmem_limit_bytes=VMEM_BYTES
        ),
        name="exchange",
    )(material, diffusivity, variation)
    return pl.pallas_call(
        write_kernel,
        out_shape=jax.ShapeDtypeStruct((27, 2, 8, 128), jnp.float32),
        in_specs=[vmem],
        out_specs=pl.BlockSpec(memory_space=pltpu.HBM),
        scratch_shapes=[pltpu.SemaphoreType.DMA((1,))],
        compiler_params=pltpu.CompilerParams(vmem_limit_bytes=VMEM_BYTES),
        name="write",
    )(result)


def solution(mesh):
    placed = (P("gz", "xy", None), P(), P("gz", "xy", None))
    return jax.shard_map(
        per_device, mesh=mesh, in_specs=placed, out_specs=P(None, "gz", "xy", None), check_vma=False
    )
```

time: 14.3 us -> 13.9 us (0.972)
  Pallas kernels: 14.1 us -> 13.8 us
    pallas_call x2, Pallas kernels: 14.1 us -> 13.8 us  [the longest x1 13.1 us: per_device(): pl.pallas_call(exchange_kernel, out_shape=jax.ShapeDtypeStruct((27, 2, 8,...]
where the time goes in v5:
time: 13.9 us; the launch traced here: 13.8 us
  Pallas kernels  13.8 us (99%)
    pallas_call x1, Pallas kernels, per_device(): pl.pallas_call(exchange_kernel, out_shape=jax.ShapeDtypeStruct((27, 2, 8,...  13.1 us
    pallas_call x1, Pallas kernels, per_device(): pl.pallas_call(write_kernel, out_shape=jax.ShapeDtypeStruct((27, 2, 8, 12...  0.7 us

profile of v5, /device:TPU:58, one launch (start us, length us, event | category | flops | bytes accessed | tf_op | source)
XLA Modules:
  0.0 13.8 jit_solution(15812693552847063727)
XLA Ops:
  0.0 13.1 %exchange.1.result = f32[27,2,8,128]{3,2,1,0:T(8,128)S(1)} custom-call(s32[4,16,256]{2,1,0:T(8,128)} %material.1, f32[8]{0:T(128)} %diffusivity.1, f32[4,16,256]{2,1,0:T(8,128)} %variation.1), custom_call_target="tpu_custom_call" | custom-call | tf_op jit(solution)/shard_map/exchange/pallas_call | solution.py:645
  13.1 0.7 %write.1 = f32[27,2,8,128]{3,2,1,0:T(8,128)} custom-call(f32[27,2,8,128]{3,2,1,0:T(8,128)S(1)} %exchange.1.result), custom_call_target="tpu_custom_call" | custom-call | tf_op jit(solution)/shard_map/write/pallas_call | solution.py:676

commit v6 on v5

--- a/solution.py
+++ b/solution.py
@@ -369,7 +369,7 @@
 
 SENT = {-1: (0, 1), 0: (0, 4), 1: (2, 2)}
 LANDED = {-1: 6, 0: 2, 1: 0}
-AHEAD = [(-1, 1), (1, 1), (0, 1)]
+AHEAD = [(-1, 1), (0, 1), (1, 1)]
 SIDE = [(-1, 0), (1, 0)]
 BACK = [(0, -1), (-1, -1), (1, -1)]
 MESSAGES = AHEAD + SIDE + BACK
@@ -475,9 +475,10 @@
     @pl.when(last)
     def _():
         pl.semaphore_wait(barrier, z_sides + 1)
+        send(*AHEAD[0])
         for dz, dx in AHEAD:
             greet(here, dz, dx)
-        for dz, dx in AHEAD:
+        for dz, dx in AHEAD[1:]:
             send(dz, dx)
         for dz, dx in BACK:
             greet(barrier, dz, dx)
@@ -558,8 +559,8 @@
         jnp.logical_and(gz == count_z - 1, row_index() == 6),
     )
 
-    def spread(side):
-        for plane in range(7):
+    def spread(side, some):
+        for plane in some:
             which, factor = (kind[plane] for kind in edges[side])
             for yp, half in enumerate(split_lanes(resistivity(which, factor))):
                 beyond[side, yp, pl.ds(8 * plane, 8), :] = half
@@ -580,7 +581,7 @@
     def store(dz, dx, dy, plane, value):
         out[entry(dz, dx, dy), plane] = value
 
-    spread(1)
+    spread(1, range(7))
     own_part(load, packed(1, 0, xy == count_x - 1), store)
 
     @pl.when(xy == count_x - 1)
@@ -597,12 +598,13 @@
         for dz, dx in BACK:
             send(dz, dx, (blocks, facts))
 
-    @pl.when(not_last)
-    def _():
-        for dz, dx in AHEAD:
+    for dz, dx in ((0, 1), (1, 1), (-1, 1)):
+
+        @pl.when(not_last)
+        def _():
             receive(dz, dx)
 
-    spread(0)
+        spread(0, range(LANDED[dz], LANDED[dz] + SENT[dz][1]))
     even_next = [tiles[0, yp, pl.ds(0, 8, stride=8), :] for yp in (0, 1)]
 
     def merge(dz, dx, dy, value, rows):

time: 13.9 us -> 13.9 us (level)
  no operation moved by 1% of the time
where the time goes in v6:
time: 13.9 us; the launch traced here: 13.7 us
  Pallas kernels  13.7 us (99%)
    pallas_call x1, Pallas kernels, per_device(): pl.pallas_call(exchange_kernel, out_shape=jax.ShapeDtypeStruct((27, 2, 8,...  13 us
    pallas_call x1, Pallas kernels, per_device(): pl.pallas_call(write_kernel, out_shape=jax.ShapeDtypeStruct((27, 2, 8, 12...  0.7 us

profile of v6, /device:TPU:58, one launch (start us, length us, event | category | flops | bytes accessed | tf_op | source)
XLA Modules:
  0.0 13.7 jit_solution(10251423540275115996)
XLA Ops:
  0.0 13.0 %exchange.1.result = f32[27,2,8,128]{3,2,1,0:T(8,128)S(1)} custom-call(s32[4,16,256]{2,1,0:T(8,128)} %material.1, f32[8]{0:T(128)} %diffusivity.1, f32[4,16,256]{2,1,0:T(8,128)} %variation.1), custom_call_target="tpu_custom_call" | custom-call | tf_op jit(solution)/shard_map/exchange/pallas_call | solution.py:647
  13.0 0.7 %write.1 = f32[27,2,8,128]{3,2,1,0:T(8,128)} custom-call(f32[27,2,8,128]{3,2,1,0:T(8,128)S(1)} %exchange.1.result), custom_call_target="tpu_custom_call" | custom-call | tf_op jit(solution)/shard_map/write/pallas_call | solution.py:678

commit v7 on v5

--- a/solution.py
+++ b/solution.py
@@ -518,7 +518,7 @@
 
     def place(plane, which, factor):
         for yp, half in enumerate(split_lanes(resistivity(which, factor))):
-            split[plane, yp] = half
+            split[plane, yp, pl.ds(0, 16), :] = half
             for xp in (0, 1):
                 rows = split[plane, yp, pl.ds(xp, 8, stride=2), :]
                 tiles[xp, yp, pl.ds(8 * plane, 8), :] = rows
@@ -660,9 +660,9 @@
                 [pltpu.VMEM((7, 8, 256), kind) for kind in (jnp.int32, jnp.float32)]
                 for _ in range(2)
             ],
-            pltpu.VMEM((7, 2, 16, 128), jnp.float32),
+            pltpu.VMEM((7, 2, 24, 128), jnp.float32),
             pltpu.VMEM((2, 2, 64, 128), jnp.float32),
-            pltpu.VMEM((2, 2, 64, 128), jnp.float32),
+            pltpu.VMEM((2, 2, 72, 128), jnp.float32),
             pltpu.SemaphoreType.DMA((3,)),
             pltpu.SemaphoreType.DMA((len(MESSAGES), 2)),
             pltpu.SemaphoreType.DMA((len(MESSAGES), 2)),

time: 13.9 us -> 13.9 us (level)
  no operation moved by 1% of the time
where the time goes in v7:
time: 13.9 us; the launch traced here: 13.8 us
  Pallas kernels  13.8 us (99%)
    pallas_call x1, Pallas kernels, per_device(): pl.pallas_call(exchange_kernel, out_shape=jax.ShapeDtypeStruct((27, 2, 8,...  13.1 us
    pallas_call x1, Pallas kernels, per_device(): pl.pallas_call(write_kernel, out_shape=jax.ShapeDtypeStruct((27, 2, 8, 12...  0.7 us

profile of v7, /device:TPU:58, one launch (start us, length us, event | category | flops | bytes accessed | tf_op | source)
XLA Modules:
  0.0 13.8 jit_solution(7927289348680441171)
XLA Ops:
  0.0 13.1 %exchange.1.result = f32[27,2,8,128]{3,2,1,0:T(8,128)S(1)} custom-call(s32[4,16,256]{2,1,0:T(8,128)} %material.1, f32[8]{0:T(128)} %diffusivity.1, f32[4,16,256]{2,1,0:T(8,128)} %variation.1), custom_call_target="tpu_custom_call" | custom-call | tf_op jit(solution)/shard_map/exchange/pallas_call | solution.py:645
  13.1 0.7 %write.1 = f32[27,2,8,128]{3,2,1,0:T(8,128)} custom-call(f32[27,2,8,128]{3,2,1,0:T(8,128)S(1)} %exchange.1.result), custom_call_target="tpu_custom_call" | custom-call | tf_op jit(solution)/shard_map/write/pallas_call | solution.py:676

commit v8 on v7

--- a/solution.py
+++ b/solution.py
@@ -42,7 +42,7 @@
 
 
 def inverse(value):
-    return 1.0 / value
+    return pltpu.reciprocal(value, approx=True)
 
 
 class Group:
@@ -384,6 +384,7 @@
     facts,
     levels,
     borders,
+    low_rows,
     edges,
     split,
     tiles,
@@ -418,9 +419,13 @@
             if dx == 0:
                 target = borders[which].at[pl.ds(0 if dz > 0 else 2, planes)]
             else:
-                row, rows, at = (14, 2, 6) if dx > 0 else (0, 1, 0)
+                row, rows = (14, 2) if dx > 0 else (0, 1)
                 source = origin[which].at[pl.ds(first, planes), pl.ds(row, rows)]
-                target = edges[0 if dx > 0 else 1][which].at[pl.ds(LANDED[dz], planes), pl.ds(at, rows)]
+                landing = pl.ds(LANDED[dz], planes)
+                if dx > 0:
+                    target = low_rows[which].at[landing]
+                else:
+                    target = edges[which].at[landing, pl.ds(0, 1)]
             made.append(
                 pltpu.make_async_remote_copy(
                     src_ref=source,
@@ -475,9 +480,10 @@
     @pl.when(last)
     def _():
         pl.semaphore_wait(barrier, z_sides + 1)
+        send(*AHEAD[0])
         for dz, dx in AHEAD:
             greet(here, dz, dx)
-        for dz, dx in AHEAD:
+        for dz, dx in AHEAD[1:]:
             send(dz, dx)
         for dz, dx in BACK:
             greet(barrier, dz, dx)
@@ -514,7 +520,7 @@
                 jnp.where(chosen, values[2 * n + 1], values[2 * n])
                 for n in range(len(values) // 2)
             ]
-        return -0.5 / (values[0] * factor)
+        return -0.5 * inverse(values[0] * factor)
 
     def place(plane, which, factor):
         for yp, half in enumerate(split_lanes(resistivity(which, factor))):
@@ -558,18 +564,19 @@
         jnp.logical_and(gz == count_z - 1, row_index() == 6),
     )
 
-    def spread(side):
+    def spread():
         for plane in range(7):
-            which, factor = (kind[plane] for kind in edges[side])
+            which, factor = (kind[plane] for kind in edges)
             for yp, half in enumerate(split_lanes(resistivity(which, factor))):
-                beyond[side, yp, pl.ds(8 * plane, 8), :] = half
-
-    def packed(side, row, missing):
+                beyond[yp, pl.ds(8 * plane, 8), :] = half
+
+    def bounded(halves, missing):
         missing = jnp.logical_or(outside, missing)
-        return [
-            jnp.where(missing, OUTSIDE, beyond[side, yp, pl.ds(row, 8, stride=8), :])
-            for yp in (0, 1)
-        ]
+        return [jnp.where(missing, OUTSIDE, half) for half in halves]
+
+    def low_row(row):
+        which, factor = (kind[:, row, :] for kind in low_rows)
+        return bounded(split_lanes(resistivity(which, factor)), xy == 0)
 
     def entry(dz, dx, dy):
         return 9 * (dz + 1) + 3 * (dx + 1) + dy + 1
@@ -580,8 +587,9 @@
     def store(dz, dx, dy, plane, value):
         out[entry(dz, dx, dy), plane] = value
 
-    spread(1)
-    own_part(load, packed(1, 0, xy == count_x - 1), store)
+    spread()
+    high = [beyond[yp, pl.ds(0, 8, stride=8), :] for yp in (0, 1)]
+    own_part(load, bounded(high, xy == count_x - 1), store)
 
     @pl.when(xy == count_x - 1)
     def _():
@@ -602,7 +610,6 @@
         for dz, dx in AHEAD:
             receive(dz, dx)
 
-    spread(0)
     even_next = [tiles[0, yp, pl.ds(0, 8, stride=8), :] for yp in (0, 1)]
 
     def merge(dz, dx, dy, value, rows):
@@ -613,7 +620,7 @@
             piece = value[row : row + 1, :]
             out[at] = piece if dx else out[at] + piece
 
-    edge_part(packed(0, 6, xy == 0), packed(0, 7, xy == 0), even_next, merge)
+    edge_part(low_row(0), low_row(1), even_next, merge)
 
     @pl.when(gz == 0)
     def _():
@@ -656,13 +663,11 @@
             pltpu.VMEM((4, 16, 256), jnp.float32),
             pltpu.SMEM((8,), jnp.float32),
             [pltpu.VMEM((3, 16, 256), kind) for kind in (jnp.int32, jnp.float32)],
-            [
-                [pltpu.VMEM((7, 8, 256), kind) for kind in (jnp.int32, jnp.float32)]
-                for _ in range(2)
-            ],
+            [pltpu.VMEM((8, 2, 256), kind) for kind in (jnp.int32, jnp.float32)],
+            [pltpu.VMEM((7, 8, 256), kind) for kind in (jnp.int32, jnp.float32)],
             pltpu.VMEM((7, 2, 24, 128), jnp.float32),
             pltpu.VMEM((2, 2, 64, 128), jnp.float32),
-            pltpu.VMEM((2, 2, 72, 128), jnp.float32),
+            pltpu.VMEM((2, 72, 128), jnp.float32),
             pltpu.SemaphoreType.DMA((3,)),
             pltpu.SemaphoreType.DMA((len(MESSAGES), 2)),
             pltpu.SemaphoreType.DMA((len(MESSAGES), 2)),

time: 13.9 us -> 13.9 us (level)
  no operation moved by 1% of the time
where the time goes in v8:
time: 13.9 us; the launch traced here: 13.8 us
  Pallas kernels  13.7 us (99%)
    pallas_call x1, Pallas kernels, per_device(): pl.pallas_call(exchange_kernel, out_shape=jax.ShapeDtypeStruct((27, 2, 8,...  13.1 us
    pallas_call x1, Pallas kernels, per_device(): pl.pallas_call(write_kernel, out_shape=jax.ShapeDtypeStruct((27, 2, 8, 12...  0.7 us

profile of v8, /device:TPU:58, one launch (start us, length us, event | category | flops | bytes accessed | tf_op | source)
XLA Modules:
  0.0 13.8 jit_solution(6924919513981132538)
XLA Ops:
  0.0 13.1 %exchange.1.result = f32[27,2,8,128]{3,2,1,0:T(8,128)S(1)} custom-call(s32[4,16,256]{2,1,0:T(8,128)} %material.1, f32[8]{0:T(128)} %diffusivity.1, f32[4,16,256]{2,1,0:T(8,128)} %variation.1), custom_call_target="tpu_custom_call" | custom-call | tf_op jit(solution)/shard_map/exchange/pallas_call | solution.py:652
  13.1 0.7 %write.1 = f32[27,2,8,128]{3,2,1,0:T(8,128)} custom-call(f32[27,2,8,128]{3,2,1,0:T(8,128)S(1)} %exchange.1.result), custom_call_target="tpu_custom_call" | custom-call | tf_op jit(solution)/shard_map/write/pallas_call | solution.py:681
